TPU v7x, 32 devices: a whole 2x2x4 slice. The times are simulated.
32 devices in a mesh: req: 8 (over y, x, core), mlp: 4 (over z).
Axes of the slice: x: 2, y: 2, z: 4, core: 2. Of those that a mesh axis runs over, the one named last changes fastest.
Arguments:
- tokens: bfloat16 [4096, 1024], P(('req', 'mlp')), may hold values from -6 to 6
- token_owner: int32 [4096, 1], replicated, may hold values from 0 to 31; in each aligned block of 128 rows (0 to 127, 128 to 255, ...) at most 8 rows name the same one
- token_request: int32 [4096], replicated, may hold values from 0 to 3
- cache_len: int32 [128], P(('req', 'mlp')), may hold values from 1 to 512, 32768 in all
- cache_k: bfloat16 [128, 512, 1024], P(('req', 'mlp')), may hold values from -6 to 6
- cache_v: bfloat16 [128, 512, 1024], P(('req', 'mlp')), may hold values from -12 to 12
- w_qkv: bfloat16 [1024, 3072], replicated, may hold values from -0.1875 to 0.1875
- w_out: bfloat16 [1024, 1024], replicated, may hold values from -0.375 to 0.375
- w_fc1: bfloat16 [1024, 4096], P(None, 'mlp'), may hold values from -0.1875 to 0.1875
- w_fc2: bfloat16 [4096, 1024], P('mlp'), may hold values from -0.09375 to 0.09375
- ln1_gain: float32 [1024], replicated, may hold values from 0.1 to 1.9
- ln1_bias: float32 [1024], replicated, may hold values from -3 to 3
- ln2_gain: float32 [1024], replicated, may hold values from 0.1 to 1.9
- ln2_bias: float32 [1024], replicated, may hold values from -3 to 3
Outputs:
- layer_out: bfloat16 [4096, 1024], P(('req', 'mlp'))
Inputs may be any that keep to these rules, and one draw needn't show every extreme that they name: `token_owner`: in each aligned block of 128 rows (the rows of one device) no owner is named more than 8 times, a bound that some block reaches; every owner is named somewhere. `cache_len`: some request has exactly 512 cached positions.
All inputs are finite; a program needn't handle non-finite values. No bound on the sum of `cache_len` on one device may be relied on, other than what follows from the above.
Results may differ from a plain program's by a relative error of at most 0.01.
Values may be sent and summed in bfloat16 or wider, within the bound.
No kernel may reach another device: no remote copies, remote signals or barrier semaphores. Data moves between devices by JAX's collectives and lax.ppermute only.
A program may use at most 128 MiB of HBM per device.

v0:
```python
import jax
import jax.numpy as jnp
from jax import lax
from jax.sharding import PartitionSpec as P

HEADS = 16


epsilon = 1e-05


def layer_norm(values, gain, shift):
    center = values - jnp.mean(values, axis=-1, keepdims=True)
    spread = jnp.mean(center * center, axis=-1, keepdims=True)
    return center * lax.rsqrt(spread + epsilon) * gain + shift


def slot_table(owners_flat, requests_flat, owner_index, devices, tok_dev, capacity):
    owners = owners_flat.reshape(devices, tok_dev)
    requests = requests_flat.reshape(devices, tok_dev)
    mine_mask = (owners == owner_index).astype(jnp.int32)
    ranking = jnp.cumsum(mine_mask, axis=1) - 1
    places = jnp.arange(capacity, dtype=jnp.int32)
    hit_table = mine_mask[:, :, None] * (ranking[:, :, None] == places[None, None, :]).astype(
        jnp.int32
    )
    filled = jnp.sum(hit_table, axis=1)
    positions = jnp.arange(tok_dev, dtype=jnp.int32)
    local_row = jnp.sum(hit_table * positions[None, :, None], axis=1)
    sources = jnp.arange(devices, dtype=jnp.int32)[:, None]
    global_row = jnp.where(filled > 0, sources * tok_dev + local_row, -1).reshape(-1)
    slot_request = jnp.sum(hit_table * requests[:, :, None], axis=1).reshape(-1)
    return (global_row, slot_request, filled.reshape(-1))


def attend(projections, cache_keys, cache_values, lengths, global_row, slot_request, filled):
    slot_count = projections.shape[0]
    width = projections.shape[1] // 3
    head_dim = width // HEADS
    context = cache_keys.shape[1]
    score_scale = head_dim ** (-0.5)
    queries = projections[:, :width].reshape(slot_count, HEADS, head_dim)
    key_new = projections[:, width : 2 * width].reshape(slot_count, HEADS, head_dim)
    value_new = projections[:, 2 * width :].reshape(slot_count, HEADS, head_dim)
    new_mask = (
        (filled[None, :] > 0)
        & (slot_request[None, :] == slot_request[:, None])
        & (global_row[None, :] <= global_row[:, None])
    )
    new_score = (
        jnp.einsum("rhd,shd->hrs", queries, key_new, preferred_element_type=jnp.float32)
        * score_scale
    )
    new_exp = jnp.where(new_mask[None], jnp.exp(new_score), jnp.float32(0.0))
    new_total = jnp.sum(new_exp, axis=-1)
    key_place = jnp.arange(context, dtype=jnp.int32)

    def one_request(items):
        keys_here, values_here, length, request_index = items
        mask = (slot_request[:, None] == request_index) & (key_place[None, :] < length)
        score = (
            jnp.einsum(
                "rhd,khd->hrk",
                queries,
                keys_here.reshape(context, HEADS, head_dim),
                preferred_element_type=jnp.float32,
            )
            * score_scale
        )
        old_exp = jnp.where(mask[None], jnp.exp(score), jnp.float32(0.0))
        old_total = jnp.sum(old_exp, axis=-1)
        total = old_total + new_total
        total = jnp.where(total > 0, total, jnp.float32(1.0))
        weight = (old_exp / total[:, :, None]).astype(jnp.bfloat16)
        part = jnp.einsum(
            "hrk,khd->rhd",
            weight,
            values_here.reshape(context, HEADS, head_dim),
            preferred_element_type=jnp.float32,
        )
        return (part, old_total)

    request_ids = jnp.arange(cache_keys.shape[0], dtype=jnp.int32)
    parts, totals = lax.map(one_request, (cache_keys, cache_values, lengths, request_ids))
    denominator = jnp.sum(totals, axis=0) + new_total
    denominator = jnp.where(denominator > 0, denominator, jnp.float32(1.0))
    new_weight = (new_exp / denominator[:, :, None]).astype(jnp.bfloat16)
    result = jnp.sum(parts, axis=0)
    result = result + jnp.einsum(
        "hrs,shd->rhd", new_weight, value_new, preferred_element_type=jnp.float32
    )
    return result.reshape(slot_count, width).astype(jnp.bfloat16)


def per_device(
    tokens,
    token_owner,
    token_request,
    cache_len,
    cache_k,
    cache_v,
    w_qkv,
    w_out,
    w_fc1,
    w_fc2,
    ln1_gain,
    ln1_bias,
    ln2_gain,
    ln2_bias,
):
    n_req = lax.axis_size("req")
    n_mlp = lax.axis_size("mlp")
    devices = n_req * n_mlp
    owner_index = lax.axis_index("req") * n_mlp + lax.axis_index("mlp")
    tok_dev, width = tokens.shape
    capacity = max(2, 2 * tok_dev // devices)
    slot_count = devices * capacity
    owners_flat = token_owner.reshape(-1)
    my_owners = lax.dynamic_slice_in_dim(owners_flat, owner_index * tok_dev, tok_dev)
    owner_onehot = (my_owners[:, None] == jnp.arange(devices, dtype=jnp.int32)[None, :]).astype(
        jnp.int32
    )
    ranking = jnp.cumsum(owner_onehot, axis=0) - 1
    my_rank = jnp.sum(owner_onehot * ranking, axis=1)
    column = my_owners * capacity + my_rank
    dispatch = (column[:, None] == jnp.arange(slot_count, dtype=jnp.int32)[None, :]).astype(
        jnp.bfloat16
    )
    outgoing = jnp.einsum("tr,td->rd", dispatch, tokens, preferred_element_type=jnp.float32).astype(
        jnp.bfloat16
    )
    arrived = lax.all_to_all(
        outgoing.reshape(devices, capacity, width),
        ("req", "mlp"),
        split_axis=0,
        concat_axis=0,
        tiled=True,
    )
    projections = jnp.dot(
        arrived.reshape(slot_count, width), w_qkv, preferred_element_type=jnp.float32
    ).astype(jnp.bfloat16)
    global_row, slot_request, filled = slot_table(
        owners_flat, token_request, owner_index, devices, tok_dev, capacity
    )
    attended = attend(projections, cache_k, cache_v, cache_len, global_row, slot_request, filled)
    returned = lax.all_to_all(
        attended.reshape(devices, capacity, width),
        ("req", "mlp"),
        split_axis=0,
        concat_axis=0,
        tiled=True,
    )
    attn_rows = jnp.dot(
        dispatch, returned.reshape(slot_count, width), preferred_element_type=jnp.float32
    ).astype(jnp.bfloat16)
    projected_out = jnp.dot(attn_rows, w_out, preferred_element_type=jnp.float32)
    normed = layer_norm(projected_out + tokens.astype(jnp.float32), ln1_gain, ln1_bias).astype(
        jnp.bfloat16
    )
    gathered = lax.all_gather(normed, "mlp", axis=0, tiled=True)
    hidden = jax.nn.gelu(
        jnp.dot(gathered, w_fc1, preferred_element_type=jnp.float32), approximate=False
    ).astype(jnp.bfloat16)
    summed = lax.psum_scatter(
        jnp.dot(hidden, w_fc2, preferred_element_type=jnp.float32).astype(jnp.bfloat16),
        "mlp",
        scatter_dimension=0,
        tiled=True,
    ).astype(jnp.float32)
    return layer_norm(normed.astype(jnp.float32) + summed, ln2_gain, ln2_bias).astype(jnp.bfloat16)


def solution(mesh):
    placed = (
        P(("req", "mlp"), None),
        P(),
        P(),
        P(("req", "mlp")),
        P(("req", "mlp"), None, None),
        P(("req", "mlp"), None, None),
        P(),
        P(),
        P(None, "mlp"),
        P("mlp", None),
        P(),
        P(),
        P(),
        P(),
    )
    return jax.shard_map(
        per_device, mesh=mesh, in_specs=placed, out_specs=P(("req", "mlp"), None), check_vma=False
    )
```

profile of v0, /device:TPU:0, one launch (start us, length us, event | category | flops | bytes accessed | tf_op | source)
XLA Modules:
  0.0 240.1 jit_solution(13278767428710312576)
XLA Ops:
  8.5 2.1 fusion.23
  10.6 7.3 %all-to-all-start = ((bf16[32,8,1024]{2,1,0:T(8,128)(2,1)}), bf16[32,8,1024]{2,1,0:T(8,128)(2,1)S(1)}, u32[]{:S(2)}, u32[]{:S(2)}) async-start(bf16[32,8,1024]{2,1,0:T(8,128)(2,1)} %fusion.23), calls=%async_computation | async-start | bytes 1048576 | tf_op jit(solution)/shard_map/all_to_all | solution.py:132
  18.3 1.7 fusion.61
  20.6 11.7 %all-to-all-done = bf16[32,8,1024]{2,1,0:T(8,128)(2,1)S(1)} async-done(((bf16[32,8,1024]{2,1,0:T(8,128)(2,1)}), bf16[32,8,1024]{2,1,0:T(8,128)(2,1)S(1)}, u32[]{:S(2)}, u32[]{:S(2)}) %all-to-all-start) | async-done | bytes 524320 | tf_op jit(solution)/shard_map/all_to_all | solution.py:132
  32.3 4.6 %convolution_convert_fusion = bf16[256,3072]{1,0:T(8,128)(2,1)S(1)} fusion(bf16[1024,3072]{1,0:T(8,128)(2,1)} %param.22, bf16[32,8,1024]{2,1,0:T(8,128)(2,1)S(1)} %all-to-all-done), kind=kOutput, calls=%fused_computation.18 | convolution fusion | flops 1611399168 | bytes 8388608 | tf_op jit(solution)/shard_map/dot_general | solution.py:139
  39.1 4.1 %fusion.8 = (f32[16,256]{1,0:T(8,128)S(1)}, f32[16,256,256]{1,2,0:T(8,128)}) fusion(pred[256,256]{0,1:T(8,128)(4,1)S(1)} %compare_and_fusion, bf16[256,16,64]{0,2,1:T(8,128)(2,1)} %bitcast.89, bf16[256,16,64]{0,2,1:T(8,128)(2,1)S(1)} %bitcast.92), kind=kOutput, calls=%fused_computation.19 | convolution fusion | flops 137359360 | bytes 5324800 | tf_op jit(solution)/shard_map/rhd,shd->hrs/dot_general | solution.py:51
  43.1 88.4 %while.13 = (s32[]{:T(128)}, f32[4,256,16,64]{1,3,2,0:T(8,128)}, f32[4,16,256]{2,1,0:T(8,128)S(1)}, bf16[4,512,1024]{2,1,0:T(8,128)(2,1)}, s32[4]{0:T(128)S(1)},...) while((s32[]{:T(128)}, f32[4,256,16,64]{1,3,2,0:T(8,128)}, ...), condition=%wide.region_9.10_spmd.clone, body=%wide.region_7.9_spmd.clone.sunk | while | flops 551691008 | bytes 29347476 | solution.py:84
  45.7 2.7 %constant_dynamic-slice_fusion.4 = (bf16[1,512,1024]{2,1,0:T(8,128)(2,1)}, bf16[1,512,1024]{2,1,0:T(8,128)(2,1)S(1)}) fusion(bf16[4,512,1024]{2,1,0:T(8,128)(2,1)} %get-tuple-element.249, s32[]{:T(128)} %get-tuple-element.231, bf16[4,512,1024]{2,1,0:T(8,128)(2,1)} %get-tuple-element.245), kind=kLoop, calls=%fused_computation.12.clone.1 | loop fusion | bytes 4194308 | tf_op jit(solution)/shard_map/while/body/jit(dynamic_index_in_dim)/dynamic_slice | solution.py:84
  48.4 2.3 copy.46
  50.7 6.5 %fusion.126 = (f32[16,256]{1,0:T(8,128)S(1)}, f32[16,512,256]{2,1,0:T(8,128)}) fusion(pred[256,512]{0,1:T(8,128)(4,1)S(1)} %broadcast_and_fusion.2, bf16[512,16,64]{0,2,1:T(8,128)(2,1)} %bitcast.88, bf16[256,16,64]{0,2,1:T(8,128)(2,1)} %get-tuple-element.250), kind=kOutput, calls=%fused_computation.3.clone.1 | convolution fusion | flops 274722816 | bytes 10108928 | tf_op jit(solution)/shard_map/while/body/eval_jaxpr/rhd,khd->hrk/dot_general | solution.py:62
  58.5 6.8 %fusion.127 = f32[4,256,16,64]{1,3,2,0:T(8,128)} fusion(f32[4,256,16,64]{1,3,2,0:T(8,128)} %get-tuple-element.232, s32[]{:T(128)} %get-tuple-element.231, bf16[512,16,64]{0,2,1:T(8,128)(2,1)} %bitcast.87, f32[16,512,256]{2,1,0:T(8,128)} %get-tuple-element.218, f32[16,256]{1,0:T(8,128)S(1)} %compare_select_fusion.3, ...), kind=kOutput, calls=%fused_computation.6.clone.1 | convolution fusion | flops 276824064 | bytes 10633728 | tf_op jit(solution)/shard_map/while/body/eval_jaxpr/hrk,khd->rhd/dot_general | solution.py:75
  67.8 2.7 %constant_dynamic-slice_fusion.4 = (bf16[1,512,1024]{2,1,0:T(8,128)(2,1)}, bf16[1,512,1024]{2,1,0:T(8,128)(2,1)S(1)}) fusion(bf16[4,512,1024]{2,1,0:T(8,128)(2,1)} %get-tuple-element.249, s32[]{:T(128)} %get-tuple-element.231, bf16[4,512,1024]{2,1,0:T(8,128)(2,1)} %get-tuple-element.245), kind=kLoop, calls=%fused_computation.12.clone.1 | loop fusion | bytes 4194308 | tf_op jit(solution)/shard_map/while/body/jit(dynamic_index_in_dim)/dynamic_slice | solution.py:84
  70.6 2.3 copy.46
  72.8 6.5 %fusion.126 = (f32[16,256]{1,0:T(8,128)S(1)}, f32[16,512,256]{2,1,0:T(8,128)}) fusion(pred[256,512]{0,1:T(8,128)(4,1)S(1)} %broadcast_and_fusion.2, bf16[512,16,64]{0,2,1:T(8,128)(2,1)} %bitcast.88, bf16[256,16,64]{0,2,1:T(8,128)(2,1)} %get-tuple-element.250), kind=kOutput, calls=%fused_computation.3.clone.1 | convolution fusion | flops 274722816 | bytes 10108928 | tf_op jit(solution)/shard_map/while/body/eval_jaxpr/rhd,khd->hrk/dot_general | solution.py:62
  80.7 6.7 %fusion.127 = f32[4,256,16,64]{1,3,2,0:T(8,128)} fusion(f32[4,256,16,64]{1,3,2,0:T(8,128)} %get-tuple-element.232, s32[]{:T(128)} %get-tuple-element.231, bf16[512,16,64]{0,2,1:T(8,128)(2,1)} %bitcast.87, f32[16,512,256]{2,1,0:T(8,128)} %get-tuple-element.218, f32[16,256]{1,0:T(8,128)S(1)} %compare_select_fusion.3, ...), kind=kOutput, calls=%fused_computation.6.clone.1 | convolution fusion | flops 276824064 | bytes 10633728 | tf_op jit(solution)/shard_map/while/body/eval_jaxpr/hrk,khd->rhd/dot_general | solution.py:75
  89.9 2.7 %constant_dynamic-slice_fusion.4 = (bf16[1,512,1024]{2,1,0:T(8,128)(2,1)}, bf16[1,512,1024]{2,1,0:T(8,128)(2,1)S(1)}) fusion(bf16[4,512,1024]{2,1,0:T(8,128)(2,1)} %get-tuple-element.249, s32[]{:T(128)} %get-tuple-element.231, bf16[4,512,1024]{2,1,0:T(8,128)(2,1)} %get-tuple-element.245), kind=kLoop, calls=%fused_computation.12.clone.1 | loop fusion | bytes 4194308 | tf_op jit(solution)/shard_map/while/body/jit(dynamic_index_in_dim)/dynamic_slice | solution.py:84
  92.6 2.3 copy.46
  94.9 6.5 %fusion.126 = (f32[16,256]{1,0:T(8,128)S(1)}, f32[16,512,256]{2,1,0:T(8,128)}) fusion(pred[256,512]{0,1:T(8,128)(4,1)S(1)} %broadcast_and_fusion.2, bf16[512,16,64]{0,2,1:T(8,128)(2,1)} %bitcast.88, bf16[256,16,64]{0,2,1:T(8,128)(2,1)} %get-tuple-element.250), kind=kOutput, calls=%fused_computation.3.clone.1 | convolution fusion | flops 274722816 | bytes 10108928 | tf_op jit(solution)/shard_map/while/body/eval_jaxpr/rhd,khd->hrk/dot_general | solution.py:62
  102.8 6.7 %fusion.127 = f32[4,256,16,64]{1,3,2,0:T(8,128)} fusion(f32[4,256,16,64]{1,3,2,0:T(8,128)} %get-tuple-element.232, s32[]{:T(128)} %get-tuple-element.231, bf16[512,16,64]{0,2,1:T(8,128)(2,1)} %bitcast.87, f32[16,512,256]{2,1,0:T(8,128)} %get-tuple-element.218, f32[16,256]{1,0:T(8,128)S(1)} %compare_select_fusion.3, ...), kind=kOutput, calls=%fused_computation.6.clone.1 | convolution fusion | flops 276824064 | bytes 10633728 | tf_op jit(solution)/shard_map/while/body/eval_jaxpr/hrk,khd->rhd/dot_general | solution.py:75
  112.0 2.7 %constant_dynamic-slice_fusion.4 = (bf16[1,512,1024]{2,1,0:T(8,128)(2,1)}, bf16[1,512,1024]{2,1,0:T(8,128)(2,1)S(1)}) fusion(bf16[4,512,1024]{2,1,0:T(8,128)(2,1)} %get-tuple-element.249, s32[]{:T(128)} %get-tuple-element.231, bf16[4,512,1024]{2,1,0:T(8,128)(2,1)} %get-tuple-element.245), kind=kLoop, calls=%fused_computation.12.clone.1 | loop fusion | bytes 4194308 | tf_op jit(solution)/shard_map/while/body/jit(dynamic_index_in_dim)/dynamic_slice | solution.py:84
  114.7 2.3 copy.46
  117.0 6.5 %fusion.126 = (f32[16,256]{1,0:T(8,128)S(1)}, f32[16,512,256]{2,1,0:T(8,128)}) fusion(pred[256,512]{0,1:T(8,128)(4,1)S(1)} %broadcast_and_fusion.2, bf16[512,16,64]{0,2,1:T(8,128)(2,1)} %bitcast.88, bf16[256,16,64]{0,2,1:T(8,128)(2,1)} %get-tuple-element.250), kind=kOutput, calls=%fused_computation.3.clone.1 | convolution fusion | flops 274722816 | bytes 10108928 | tf_op jit(solution)/shard_map/while/body/eval_jaxpr/rhd,khd->hrk/dot_general | solution.py:62
  124.9 6.7 %fusion.127 = f32[4,256,16,64]{1,3,2,0:T(8,128)} fusion(f32[4,256,16,64]{1,3,2,0:T(8,128)} %get-tuple-element.232, s32[]{:T(128)} %get-tuple-element.231, bf16[512,16,64]{0,2,1:T(8,128)(2,1)} %bitcast.87, f32[16,512,256]{2,1,0:T(8,128)} %get-tuple-element.218, f32[16,256]{1,0:T(8,128)S(1)} %compare_select_fusion.3, ...), kind=kOutput, calls=%fused_computation.6.clone.1 | convolution fusion | flops 276824064 | bytes 10633728 | tf_op jit(solution)/shard_map/while/body/eval_jaxpr/hrk,khd->rhd/dot_general | solution.py:75
  131.6 3.7 %reduce_sum.116 = f32[256,16,64]{0,2,1:T(8,128)} reduce(f32[4,256,16,64]{1,3,2,0:T(8,128)} %get-tuple-element.63, f32[]{:T(128)} %constant.63.clone.1), dimensions={0}, to_apply=%region_10.11 | reduce | flops 786432 | bytes 5242884 | tf_op jit(solution)/shard_map/reduce_sum | solution.py:88
  135.5 4.4 %fusion.22 = bf16[256,16,64]{0,2,1:T(8,128)(2,1)} fusion(f32[256,16,64]{0,2,1:T(8,128)} %reduce_sum.116, bf16[256,16,64]{0,2,1:T(8,128)(2,1)S(1)} %bitcast.91, f32[16,256,256]{1,2,0:T(8,128)} %get-tuple-element.148, f32[16,256]{1,0:T(8,128)S(1)} %compare_select_fusion.1, pred[256,256]{0,1:T(8,128)(4,1)S(1)} %compare_and_fusion), kind=kOutput, calls=%fused_computation.43 | convolution fusion | flops 138936320 | bytes 6373376 | tf_op jit(solution)/shard_map/hrs,shd->rhd/dot_general | solution.py:89
  139.9 2.0 copy.38
  143.4 18.4 %all_to_all.10 = bf16[32,8,1024]{2,1,0:T(8,128)(2,1)S(1)} all-to-all(bf16[32,8,1024]{2,1,0:T(8,128)(2,1)} %convert_element_type.69), channel_id=1, replica_groups=mesh['req'=8,'mlp'=4] {'req','mlp'}, dimensions={0} | all-to-all | bytes 1048576 | tf_op jit(solution)/shard_map/all_to_all | solution.py:146
  161.9 2.3 fusion.101
  165.6 27.3 %all-gather.2.cloned.1.call-done = bf16[512,1024]{1,0:T(8,128)(2,1)} async-done(((bf16[128,1024]{1,0:T(8,128)(2,1)}), bf16[512,1024]{1,0:T(8,128)(2,1)}) %all-gather.2.cloned.1.call-update) | async-done | bytes 1048592 | tf_op jit(solution)/shard_map/all_gather | solution.py:160
  192.9 9.2 %convolution_convert_fusion.1 = bf16[512,1024]{1,0:T(8,128)(2,1)} fusion(bf16[1024,1024]{1,0:T(8,128)(2,1)S(1)} %copy-done, bf16[512,1024]{1,0:T(8,128)(2,1)} %all-gather.2.cloned.1.call-done, bf16[1024,1024]{1,0:T(8,128)(2,1)} %param.24), kind=kOutput, calls=%fused_computation.40 | convolution fusion | flops 2182086656 | bytes 6291456 | tf_op jit(solution)/shard_map/dot_general | solution.py:165
  202.1 26.8 %reduce-scatter.2.cloned.1.call-done = bf16[128,1024]{1,0:T(8,128)(2,1)} async-done(((bf16[512,1024]{1,0:T(8,128)(2,1)}), bf16[128,1024]{1,0:T(8,128)(2,1)}) %reduce-scatter.2.cloned.1.call-update) | async-done | bytes 262160 | tf_op jit(solution)/shard_map/reduce_scatter | solution.py:164
  231.4 1.9 add_convert_fusion
  (94 shorter events, 26.1 us)
Async XLA Ops:
  6.5 186.3 %copy-start = (bf16[1024,1024]{1,0:T(8,128)(2,1)S(1)}, bf16[1024,1024]{1,0:T(8,128)(2,1)}, u32[]{:S(2)}) copy-start(bf16[1024,1024]{1,0:T(8,128)(2,1)} %param.25) | copy-start | bytes 6291460
  6.5 11.4 %copy-start.5 = (s32[4096,1]{0,1:T(1,128)S(1)}, s32[4096,1]{0,1:T(1,128)}, u32[]{:S(2)}) copy-start(s32[4096,1]{0,1:T(1,128)} %param.17) | copy-start | bytes 49156
  6.5 11.7 %copy-start.6 = (s32[4096]{0:T(1024)S(1)}, s32[4096]{0:T(1024)}, u32[]{:S(2)}) copy-start(s32[4096]{0:T(1024)} %param.18) | copy-start | bytes 49156
  10.6 21.7 %all-to-all-start = ((bf16[32,8,1024]{2,1,0:T(8,128)(2,1)}), bf16[32,8,1024]{2,1,0:T(8,128)(2,1)S(1)}, u32[]{:S(2)}, u32[]{:S(2)}) async-start(bf16[32,8,1024]{2,1,0:T(8,128)(2,1)} %fusion.23), calls=%async_computation | async-start | bytes 1048576 | tf_op jit(solution)/shard_map/all_to_all | solution.py:132
  17.9 175.0 %all-gather.2.cloned.1.call-start = ((), (), s32[]{:S(2)}) async-start(), calls=%async_computation.3 | async-start | bytes 1310720 | tf_op jit(solution)/shard_map/all_gather | solution.py:160
  39.0 4.1 %copy-start.9 = (s32[4]{0:T(128)S(1)}, s32[4]{0:T(128)}, u32[]{:S(2)}) copy-start(s32[4]{0:T(128)} %param.19) | copy-start | bytes 52
  131.6 3.7 %copy-start.1 = (bf16[256,1024]{1,0:T(8,128)(2,1)S(1)}, bf16[256,1024]{1,0:T(8,128)(2,1)}, u32[]{:S(2)}) copy-start(bf16[256,1024]{1,0:T(8,128)(2,1)} %get-tuple-element.144) | copy-start | bytes 1572868
  139.9 22.0 %copy-start.2 = (bf16[128,1024]{1,0:T(8,128)(2,1)S(1)}, bf16[128,1024]{1,0:T(8,128)(2,1)}, u32[]{:S(2)}) copy-start(bf16[128,1024]{1,0:T(8,128)(2,1)} %param.16) | copy-start | bytes 786436
  161.9 2.5 %copy-start.3 = (f32[1024]{0:T(1024)S(1)}, f32[1024]{0:T(1024)}, u32[]{:S(2)}) copy-start(f32[1024]{0:T(1024)} %param.27) | copy-start | bytes 12292
  161.9 2.5 %copy-start.4 = (f32[1024]{0:T(1024)S(1)}, f32[1024]{0:T(1024)}, u32[]{:S(2)}) copy-start(f32[1024]{0:T(1024)} %param.26) | copy-start | bytes 12292
  165.3 63.6 %reduce-scatter.2.cloned.1.call-start = ((), (), s32[]{:S(2)}) async-start(), calls=%async_computation.4 | async-start | bytes 1310720 | tf_op jit(solution)/shard_map/reduce_scatter | solution.py:164
  202.0 29.3 %copy-start.7 = (f32[1024]{0:T(1024)S(1)}, f32[1024]{0:T(1024)}, u32[]{:S(2)}) copy-start(f32[1024]{0:T(1024)} %param.29) | copy-start | bytes 12292
  202.0 29.3 %copy-start.8 = (f32[1024]{0:T(1024)S(1)}, f32[1024]{0:T(1024)}, u32[]{:S(2)}) copy-start(f32[1024]{0:T(1024)} %param.28) | copy-start | bytes 12292
Sparse Core Ops, SparseCore 0:
  165.4 27.4 all-gather.1
  202.2 26.6 reduce-scatter.1
where the time goes:
time: 241 us; the launch traced here: 240 us
  matrix products  79.5 us (33%)
  waiting for transfers between devices  65.8 us (27%)
  local copies, waits for them, and re-layouts  37.4 us (16%)
  blocking collectives  18.4 us (8%)
  other arithmetic  17.6 us (7%)
  between operations  13.6 us (6%)
  starting transfers between devices  7.6 us (3%)
    dynamic_slice x20, local copies, waits for them, and re-layouts, attend(): lax.map(one_request, (cache_keys, cache_values, lengths, request_ids))  30 us
    all_gather x1, waiting for transfers between devices, per_device(): gathered = lax.all_gather(normed, 'mlp', axis=0, tiled=True)  27.3 us
    reduce_scatter x1, waiting for transfers between devices, per_device(): lax.psum_scatter(jnp.dot(hidden, w_fc2, preferred_element_type=jnp.float3...  26.8 us
    dot_general x4, matrix products, one_request(): jnp.einsum('hrk,khd->rhd', weight, values_here.reshape(context, HEADS, he...  26.8 us
    dot_general x4, matrix products, one_request(): jnp.einsum('rhd,khd->hrk', queries, keys_here.reshape(context, HEADS, hea...  26.1 us
    all_to_all x1, blocking collectives, per_device(): lax.all_to_all(attended.reshape(devices, capacity, width), ('req', 'mlp')...  18.4 us
    all_to_all x1, waiting for transfers between devices, per_device(): lax.all_to_all(outgoing.reshape(devices, capacity, width), ('req', 'mlp')...  11.7 us
    dot_general x1, matrix products, per_device(): jnp.dot(hidden, w_fc2, preferred_element_type=jnp.float32)  9.17 us
  transfers between devices with their start and end apart: 3, of which 3 were waited for; matrix products, arithmetic and copies ran while one was open for 1% of the time, Pallas kernels for 0%

commit v1 on v0

v1 whole, which is shorter than its diff:
```python
import functools

import jax
import jax.numpy as jnp
from jax import lax
from jax.experimental import pallas as pl
from jax.experimental.pallas import tpu as pltpu
from jax.sharding import PartitionSpec as P

HEADS = 16
GROUP = 4
TILE = 64
MASKED = -1e30
VMEM_LIMIT = 56 * 1024 * 1024

epsilon = 1e-05


def layer_norm(values, gain, shift):
    center = values - jnp.mean(values, axis=-1, keepdims=True)
    spread = jnp.mean(center * center, axis=-1, keepdims=True)
    return center * lax.rsqrt(spread + epsilon) * gain + shift


def iota(shape, dim):
    return lax.broadcasted_iota(jnp.int32, shape, dim)


def own_pairs(owners_ref, me):
    tok_dev = owners_ref.shape[1]
    across = jnp.broadcast_to(owners_ref[pl.ds(me, 1), :], (tok_dev, tok_dev)).astype(jnp.float32)
    return across, across.T


def dispatch_kernel(capacity, me_ref, owners_ref, tokens_ref, out_ref):
    tok_dev = tokens_ref.shape[0]
    slots = out_ref.shape[0]
    across, down = own_pairs(owners_ref, me_ref[0])
    square = (tok_dev, tok_dev)
    earlier = (across == down) & (iota(square, 0) < iota(square, 1))
    rank = jnp.sum(jnp.where(earlier, 1.0, 0.0), axis=0, keepdims=True)
    column = across[:1, :] * capacity + rank
    onehot = iota((slots, tok_dev), 0).astype(jnp.float32) == column
    onehot = jnp.where(onehot, 1.0, 0.0).astype(jnp.bfloat16)
    out_ref[...] = jnp.dot(
        onehot, tokens_ref[...], preferred_element_type=jnp.float32
    ).astype(jnp.bfloat16)


def table_kernel(
    capacity, me_ref, owners_ref, requests_ref, back_ref, sort_ref, unsort_ref, starts_ref
):
    devices, tok_dev = owners_ref.shape
    slots = sort_ref.shape[0]
    me = me_ref[0]
    across, down = own_pairs(owners_ref, me)
    square = (tok_dev, tok_dev)
    earlier = (across == down) & (iota(square, 1) < iota(square, 0))
    rank = jnp.sum(jnp.where(earlier, 1.0, 0.0), axis=1, keepdims=True)
    column = down[:, :1] * capacity + rank
    back = iota((tok_dev, slots), 1).astype(jnp.float32) == column
    back_ref[...] = jnp.where(back, 1.0, 0.0).astype(jnp.bfloat16)
    mine = owners_ref[...] == me
    before = jnp.where(iota(square, 0) < iota(square, 1), 1.0, 0.0).astype(jnp.bfloat16)
    ranking = jnp.dot(
        jnp.where(mine, 1.0, 0.0).astype(jnp.bfloat16), before, preferred_element_type=jnp.float32
    ).astype(jnp.bfloat16)
    coded = jnp.where(mine, requests_ref[...] + 1, 0).astype(jnp.float32).astype(jnp.bfloat16)
    slot = iota((slots, devices), 0)
    source = iota((slots, devices), 1)
    from_here = (slot >= source * capacity) & (slot < (source + 1) * capacity)
    place = jnp.sum(jnp.where(from_here, slot - source * capacity, 0), axis=1, keepdims=True)
    from_here = jnp.where(from_here, 1.0, 0.0).astype(jnp.bfloat16)
    rank_of = jnp.dot(from_here, ranking, preferred_element_type=jnp.float32)
    code_of = jnp.dot(from_here, coded, preferred_element_type=jnp.float32)
    hit = rank_of == place.astype(jnp.float32)
    code = jnp.sum(jnp.where(hit, code_of, 0.0), axis=1, keepdims=True)
    wide = (slots, slots)
    code_i = jnp.broadcast_to(code, wide)
    code_j = code_i.T
    sub, lane = iota(wide, 0), iota(wide, 1)
    ahead_j = (code_j > 0) & ((code_j < code_i) | ((code_j == code_i) & (lane < sub)))
    ahead_i = (code_i > 0) & ((code_i < code_j) | ((code_i == code_j) & (sub < lane)))
    place_i = jnp.sum(jnp.where(ahead_j, 1.0, 0.0), axis=1, keepdims=True)
    place_j = jnp.sum(jnp.where(ahead_i, 1.0, 0.0), axis=0, keepdims=True)
    sort = (place_j == sub.astype(jnp.float32)) & (code_j > 0)
    unsort = (place_i == lane.astype(jnp.float32)) & (code_i > 0)
    sort_ref[...] = jnp.where(sort, 1.0, 0.0).astype(jnp.bfloat16)
    unsort_ref[...] = jnp.where(unsort, 1.0, 0.0).astype(jnp.bfloat16)
    few = code_j[:8, :]
    upto = (few > 0) & (few <= iota((8, slots), 0).astype(jnp.float32))
    starts = jnp.sum(jnp.where(upto, 1.0, 0.0), axis=1, keepdims=True)
    starts_ref[...] = jnp.broadcast_to(starts, starts_ref.shape).astype(jnp.int32)


def attend_kernel(
    starts_ref,
    lengths_ref,
    sort_ref,
    unsort_ref,
    x_ref,
    w_ref,
    keys_ref,
    values_ref,
    out_ref,
    sorted_ref,
    proj_ref,
    att_ref,
):
    slots, width = x_ref.shape
    requests, context, _ = keys_ref.shape
    head_dim = width // HEADS
    span = GROUP * head_dim
    scale = head_dim ** (-0.5)
    sorted_ref[...] = jnp.dot(
        sort_ref[...], x_ref[...], preferred_element_type=jnp.float32
    ).astype(jnp.bfloat16)
    att_ref[...] = jnp.zeros_like(att_ref)

    @pl.loop(0, 3 * width // span)
    def _(c):
        columns = pl.ds(pl.multiple_of(c * span, span), span)
        proj_ref[:, columns] = jnp.dot(
            sorted_ref[...], w_ref[:, columns], preferred_element_type=jnp.float32
        ).astype(jnp.bfloat16)

    starts = [starts_ref[r, 0] for r in range(requests + 1)]
    filled = starts[requests]

    @pl.loop(0, pl.cdiv(filled, TILE))
    def _(t):
        first = pl.multiple_of(t * TILE, TILE)
        rows = pl.ds(first, TILE)
        last = jnp.minimum(first + TILE, filled) - 1
        low = sum((starts[r] <= first).astype(jnp.int32) for r in range(1, requests))
        high = sum((starts[r] <= last).astype(jnp.int32) for r in range(1, requests))

        @pl.loop(low, high + 1)
        def _(r):
            begin, end = starts_ref[r, 0], starts_ref[r + 1, 0]

            @pl.when(end > begin)
            def _():
                row = iota((TILE, 1), 0) + first
                in_request = (row >= begin) & (row < end)
                key = iota((1, slots), 1)
                seen = (key >= begin) & (key <= row)
                new_bias = jnp.where(seen, 0.0, MASKED)
                new_bias = jnp.concatenate([new_bias] * GROUP, axis=0)
                valid = iota((1, context), 1) < lengths_ref[r]
                old_bias = jnp.where(valid, 0.0, MASKED)
                head_of = iota((1, span), 1) // head_dim
                for g in range(HEADS // GROUP):
                    lo = g * span
                    q = proj_ref[rows, lo : lo + span]
                    q = jnp.concatenate(
                        [jnp.where(head_of == h, q, jnp.bfloat16(0)) for h in range(GROUP)], axis=0
                    )
                    k_new = proj_ref[:, width + lo : width + lo + span]
                    v_new = proj_ref[:, 2 * width + lo : 2 * width + lo + span]
                    k_old = keys_ref[r, :, lo : lo + span]
                    v_old = values_ref[r, :, lo : lo + span]
                    across = (((1,), (1,)), ((), ()))
                    s_old = (
                        lax.dot_general(q, k_old, across, preferred_element_type=jnp.float32)
                        * scale
                        + old_bias
                    )
                    s_new = (
                        lax.dot_general(q, k_new, across, preferred_element_type=jnp.float32)
                        * scale
                        + new_bias
                    )
                    top = jnp.maximum(
                        jnp.max(s_old, axis=1, keepdims=True), jnp.max(s_new, axis=1, keepdims=True)
                    )
                    p_old = jnp.exp(s_old - top)
                    p_new = jnp.exp(s_new - top)
                    total = jnp.sum(p_old, axis=1, keepdims=True) + jnp.sum(
                        p_new, axis=1, keepdims=True
                    )
                    part = jnp.dot(
                        p_old.astype(jnp.bfloat16), v_old, preferred_element_type=jnp.float32
                    )
                    part += jnp.dot(
                        p_new.astype(jnp.bfloat16), v_new, preferred_element_type=jnp.float32
                    )
                    part = part / total
                    mixed = jnp.zeros((TILE, span), jnp.float32)
                    for h in range(GROUP):
                        mixed = jnp.where(head_of == h, part[h * TILE : (h + 1) * TILE], mixed)
                    kept = att_ref[rows, lo : lo + span]
                    att_ref[rows, lo : lo + span] = jnp.where(
                        in_request, mixed.astype(jnp.bfloat16), kept
                    )

    out_ref[...] = jnp.dot(
        unsort_ref[...], att_ref[...], preferred_element_type=jnp.float32
    ).astype(jnp.bfloat16)


def vmem(n):
    return [pl.BlockSpec(memory_space=pltpu.VMEM)] * n


def smem(n):
    return [pl.BlockSpec(memory_space=pltpu.SMEM)] * n


def params(limit=VMEM_LIMIT):
    return pltpu.CompilerParams(vmem_limit_bytes=limit)


def shape(dims, dtype=jnp.bfloat16):
    return jax.ShapeDtypeStruct(dims, dtype)


def per_device(
    tokens,
    token_owner,
    token_request,
    cache_len,
    cache_k,
    cache_v,
    w_qkv,
    w_out,
    w_fc1,
    w_fc2,
    ln1_gain,
    ln1_bias,
    ln2_gain,
    ln2_bias,
):
    n_req = lax.axis_size("req")
    n_mlp = lax.axis_size("mlp")
    devices = n_req * n_mlp
    owner_index = lax.axis_index("req") * n_mlp + lax.axis_index("mlp")
    tok_dev, width = tokens.shape
    capacity = max(2, 2 * tok_dev // devices)
    slots = devices * capacity
    me = owner_index.astype(jnp.int32).reshape(1)
    owners = token_owner.reshape(devices, tok_dev)
    requests = token_request.reshape(devices, tok_dev)
    outgoing = pl.pallas_call(
        functools.partial(dispatch_kernel, capacity),
        out_shape=shape((slots, width)),
        in_specs=smem(1) + vmem(2),
        out_specs=vmem(1)[0],
        compiler_params=params(16 * 1024 * 1024),
        name="dispatch",
    )(me, owners, tokens)
    arrived = lax.all_to_all(
        outgoing.reshape(devices, capacity, width),
        ("req", "mlp"),
        split_axis=0,
        concat_axis=0,
        tiled=True,
    )
    back, sort, unsort, starts = pl.pallas_call(
        functools.partial(table_kernel, capacity),
        out_shape=(
            shape((tok_dev, slots)),
            shape((slots, slots)),
            shape((slots, slots)),
            shape((8, 128), jnp.int32),
        ),
        in_specs=smem(1) + vmem(2),
        out_specs=tuple(vmem(4)),
        compiler_params=params(16 * 1024 * 1024),
        cost_estimate=pl.CostEstimate(flops=40_000_000, bytes_accessed=400_000, transcendentals=0),
        name="table",
    )(me, owners, requests)
    attended = pl.pallas_call(
        attend_kernel,
        out_shape=shape((slots, width)),
        in_specs=smem(2) + vmem(6),
        out_specs=vmem(1)[0],
        scratch_shapes=[
            pltpu.VMEM((slots, width), jnp.bfloat16),
            pltpu.VMEM((slots, 3 * width), jnp.bfloat16),
            pltpu.VMEM((slots, width), jnp.bfloat16),
        ],
        compiler_params=params(),
        name="attend",
    )(
        starts,
        cache_len,
        sort,
        unsort,
        arrived.reshape(slots, width),
        w_qkv,
        cache_k,
        cache_v,
    )
    returned = lax.all_to_all(
        attended.reshape(devices, capacity, width),
        ("req", "mlp"),
        split_axis=0,
        concat_axis=0,
        tiled=True,
    )
    attn_rows = jnp.dot(
        back, returned.reshape(slots, width), preferred_element_type=jnp.float32
    ).astype(jnp.bfloat16)
    projected_out = jnp.dot(attn_rows, w_out, preferred_element_type=jnp.float32)
    normed = layer_norm(projected_out + tokens.astype(jnp.float32), ln1_gain, ln1_bias).astype(
        jnp.bfloat16
    )
    gathered = lax.all_gather(normed, "mlp", axis=0, tiled=True)
    hidden = jax.nn.gelu(
        jnp.dot(gathered, w_fc1, preferred_element_type=jnp.float32), approximate=False
    ).astype(jnp.bfloat16)
    summed = lax.psum_scatter(
        jnp.dot(hidden, w_fc2, preferred_element_type=jnp.float32).astype(jnp.bfloat16),
        "mlp",
        scatter_dimension=0,
        tiled=True,
    ).astype(jnp.float32)
    return layer_norm(normed.astype(jnp.float32) + summed, ln2_gain, ln2_bias).astype(jnp.bfloat16)


def solution(mesh):
    placed = (
        P(("req", "mlp"), None),
        P(),
        P(),
        P(("req", "mlp")),
        P(("req", "mlp"), None, None),
        P(("req", "mlp"), None, None),
        P(),
        P(),
        P(None, "mlp"),
        P("mlp", None),
        P(),
        P(),
        P(),
        P(),
    )
    return jax.shard_map(
        per_device, mesh=mesh, in_specs=placed, out_specs=P(("req", "mlp"), None), check_vma=False
    )
```

time: 241 us -> 150 us (0.62)
  matrix products: 79.5 us -> 11.4 us
  local copies, waits for them, and re-layouts: 37.4 us -> 5.96 us
  Pallas kernels: 0 us -> 21.3 us
  other arithmetic: 17.6 us -> 5.53 us
    dot_general x12 -> x0, matrix products: 68 us -> none  [the longest x4 26.8 us: one_request(): jnp.einsum('hrk,khd->rhd', weight, values_here.reshape(context, HEADS, he...]
    dynamic_slice x20 -> x0, local copies, waits for them, and re-layouts: 30 us -> none  [attend(): lax.map(one_request, (cache_keys, cache_values, lengths, request_ids))]
    pallas_call x0 -> x3, Pallas kernels: none -> 21.3 us  [the longest x1 19.6 us: per_device(): pl.pallas_call(attend_kernel, out_shape=shape((slots, width)), in_specs=s...]
    unnamed x20 -> x28, local copies, waits for them, and re-layouts: 0.04 us -> 5.96 us
    reduce_sum x4 -> x0, other arithmetic: 5.52 us -> none  [the longest x1 3.65 us: attend(): result = jnp.sum(parts, axis=0)]
    convert_element_type x2 -> x0, local copies, waits for them, and re-layouts: 3.54 us -> none  [attend(): return result.reshape(slot_count, width).astype(jnp.bfloat16)]
    eq x5 -> x0, other arithmetic: 2.93 us -> none  [the longest x4 2.26 us: one_request(): slot_request[:, None] == request_index]
  transfers between devices with their start and end apart: 3 -> 3, of which waited for: 3 -> 3; matrix products, arithmetic and copies ran while one was open for 1% -> 0% of each run, Pallas kernels for 0% -> 0%
where the time goes in v1:
time: 150 us; the launch traced here: 149 us
  waiting for transfers between devices  64.7 us (43%)
  Pallas kernels  21.3 us (14%)
  blocking collectives  18.9 us (13%)
  between operations  13.5 us (9%)
  matrix products  11.4 us (8%)
  starting transfers between devices  7.38 us (5%)
  local copies, waits for them, and re-layouts  5.96 us (4%)
  other arithmetic  5.53 us (4%)
    all_gather x1, waiting for transfers between devices, per_device(): gathered = lax.all_gather(normed, 'mlp', axis=0, tiled=True)  27.5 us
    reduce_scatter x1, waiting for transfers between devices, per_device(): lax.psum_scatter(jnp.dot(hidden, w_fc2, preferred_element_type=jnp.float3...  26.8 us
    pallas_call x1, Pallas kernels, per_device(): pl.pallas_call(attend_kernel, out_shape=shape((slots, width)), in_specs=s...  19.6 us
    all_to_all x1, blocking collectives, per_device(): lax.all_to_all(attended.reshape(devices, capacity, width), ('req', 'mlp')...  18.9 us
    all_to_all x1, waiting for transfers between devices, per_device(): lax.all_to_all(outgoing.reshape(devices, capacity, width), ('req', 'mlp')...  10.4 us
    dot_general x1, matrix products, per_device(): jnp.dot(hidden, w_fc2, preferred_element_type=jnp.float32)  9.13 us
    all_to_all x1, starting transfers between devices, per_device(): lax.all_to_all(outgoing.reshape(devices, capacity, width), ('req', 'mlp')...  7.3 us
    unnamed x28, local copies, waits for them, and re-layouts  5.96 us
  transfers between devices with their start and end apart: 3, of which 3 were waited for; matrix products, arithmetic and copies ran while one was open for 0% of the time, Pallas kernels for 0%

profile of v1, /device:TPU:0, one launch (start us, length us, event | category | flops | bytes accessed | tf_op | source)
XLA Modules:
  0.0 148.7 jit_solution(3841601313986450969)
XLA Ops:
  6.5 0.0 copy-start
  6.5 1.1 copy-done.1
  7.6 0.7 copy-done.5
  8.4 1.2 dispatch.1
  9.5 7.3 %all-to-all-start = ((bf16[32,8,1024]{2,1,0:T(8,128)(2,1)}), bf16[32,8,1024]{2,1,0:T(8,128)(2,1)S(1)}, u32[]{:S(2)}, u32[]{:S(2)}) async-start(bf16[32,8,1024]{2,1,0:T(8,128)(2,1)} %bitcast.3), calls=%async_computation | async-start | bytes 1048576 | tf_op jit(solution)/shard_map/all_to_all | solution.py:252
  16.8 0.0 all-gather.2.cloned.1.call-start
  16.9 0.0 copy-start.6
  16.9 0.7 copy-done.6
  17.6 0.7 copy-done.8
  18.3 0.6 table.1
  18.9 0.0 copy-start.3
  19.0 0.6 copy-done.3
  19.6 0.7 copy-done.4
  20.3 0.6 copy-done.7
  20.8 10.4 %all-to-all-done = bf16[32,8,1024]{2,1,0:T(8,128)(2,1)S(1)} async-done(((bf16[32,8,1024]{2,1,0:T(8,128)(2,1)}), bf16[32,8,1024]{2,1,0:T(8,128)(2,1)S(1)}, u32[]{:S(2)}, u32[]{:S(2)}) %all-to-all-start) | async-done | bytes 524320 | tf_op jit(solution)/shard_map/all_to_all | solution.py:252
  31.2 0.8 copy-done.9
  32.0 19.6 %attend.1 = bf16[256,1024]{1,0:T(8,128)(2,1)} custom-call(s32[8,128]{1,0:T(8,128)} %copy-done.7, s32[4]{0:T(128)} %lengths_ref.1, bf16[256,256]{1,0:T(8,128)(2,1)} %copy-done.3, bf16[256,256]{1,0:T(8,128)(2,1)} %copy-done.4, bf16[256,1024]{1,0:T(8,128)(2,1)} %bitcast.20, bf16[1024,3072]{1,0:T(8,128)(2,1)} %w_ref.1, bf16[4,512,1024]{2,1,0:T(8,128)(2,1)} %keys_ref.1, ...), custom_call_target="tpu_custom_call" | custom-call | tf_op jit(solution)/shard_map/attend/pallas_call | solution.py:273
  51.6 18.9 %all_to_all.10 = bf16[32,8,1024]{2,1,0:T(8,128)(2,1)S(1)} all-to-all(bf16[32,8,1024]{2,1,0:T(8,128)(2,1)} %bitcast.21), channel_id=1, replica_groups=mesh['req'=8,'mlp'=4] {'req','mlp'}, dimensions={0} | all-to-all | bytes 1048576 | tf_op jit(solution)/shard_map/all_to_all | solution.py:295
  70.5 0.0 copy-done.2
  70.5 2.3 %fusion.75 = (f32[128]{0:T(128)S(1)}, f32[128,1024]{1,0:T(8,128)S(1)}) fusion(bf16[128,1024]{1,0:T(8,128)(2,1)S(1)} %copy-done.2, bf16[1024,1024]{1,0:T(8,128)(2,1)} %param.21, bf16[128,256]{1,0:T(8,128)(2,1)S(1)} %get-tuple-element.9, bf16[32,8,1024]{2,1,0:T(8,128)(2,1)S(1)} %all_to_all.10), kind=kOutput, calls=%fused_computation.94 | convolution fusion | flops 336068480 | bytes 3473920 | tf_op jit(solution)/shard_map/dot_general | solution.py:305
  72.8 0.2 multiply_reduce_fusion.1
  73.0 0.0 copy-done.10
  73.0 0.9 add_convert_fusion.1
  73.9 0.0 all-gather.2.cloned.1.call-update
  73.9 0.0 reduce-scatter.2.cloned.1.call-start
  74.0 27.5 %all-gather.2.cloned.1.call-done = bf16[512,1024]{1,0:T(8,128)(2,1)} async-done(((bf16[128,1024]{1,0:T(8,128)(2,1)}), bf16[512,1024]{1,0:T(8,128)(2,1)}) %all-gather.2.cloned.1.call-update) | async-done | bytes 1048592 | tf_op jit(solution)/shard_map/all_gather | solution.py:309
  101.5 9.1 %convolution_convert_fusion = bf16[512,1024]{1,0:T(8,128)(2,1)} fusion(bf16[1024,1024]{1,0:T(8,128)(2,1)S(1)} %copy-done, bf16[512,1024]{1,0:T(8,128)(2,1)} %all-gather.2.cloned.1.call-done, bf16[1024,1024]{1,0:T(8,128)(2,1)} %param.22), kind=kOutput, calls=%fused_computation.19 | convolution fusion | flops 2182086656 | bytes 6291456 | tf_op jit(solution)/shard_map/dot_general | solution.py:314
  110.6 0.0 reduce-scatter.2.cloned.1.call-update
  110.7 26.8 %reduce-scatter.2.cloned.1.call-done = bf16[128,1024]{1,0:T(8,128)(2,1)} async-done(((bf16[512,1024]{1,0:T(8,128)(2,1)}), bf16[128,1024]{1,0:T(8,128)(2,1)}) %reduce-scatter.2.cloned.1.call-update) | async-done | bytes 262160 | tf_op jit(solution)/shard_map/reduce_scatter | solution.py:313
  137.4 1.2 fusion.44
  138.7 1.3 multiply_reduce_fusion
  140.0 1.9 %add_convert_fusion = bf16[128,1024]{1,0:T(8,128)(2,1)} fusion(bf16[128,1024]{1,0:T(8,128)(2,1)} %reduce-scatter.2.cloned.1.call-done, f32[1024]{0:T(1024)S(1)} %copy-done.12, f32[1024]{0:T(1024)S(1)} %copy-done.13, f32[128]{0:T(128)S(1)} %add_rsqrt_fusion, f32[128]{0:T(128)S(1)} %broadcast_multiply_fusion, f32[1024]{0:T(1024)S(1)} %copy-done.10, ...), kind=kLoop, calls=%fused_computation.53 | loop fusion | flops 1703936 | bytes 1067008 | tf_op jit(solution)/shard_map/convert_element_type | solution.py:319
  (19 shorter events, 0.1 us)
Async XLA Ops:
  6.5 95.0 %copy-start = (bf16[1024,1024]{1,0:T(8,128)(2,1)S(1)}, bf16[1024,1024]{1,0:T(8,128)(2,1)}, u32[]{:S(2)}) copy-start(bf16[1024,1024]{1,0:T(8,128)(2,1)} %param.23) | copy-start | bytes 6291460
  6.5 1.1 copy-start.1
  7.6 0.7 copy-start.5
  9.5 21.7 %all-to-all-start = ((bf16[32,8,1024]{2,1,0:T(8,128)(2,1)}), bf16[32,8,1024]{2,1,0:T(8,128)(2,1)S(1)}, u32[]{:S(2)}, u32[]{:S(2)}) async-start(bf16[32,8,1024]{2,1,0:T(8,128)(2,1)} %bitcast.3), calls=%async_computation | async-start | bytes 1048576 | tf_op jit(solution)/shard_map/all_to_all | solution.py:252
  16.8 84.7 %all-gather.2.cloned.1.call-start = ((), (), s32[]{:S(2)}) async-start(), calls=%async_computation.3 | async-start | bytes 1310720 | tf_op jit(solution)/shard_map/all_gather | solution.py:309
  16.9 0.7 copy-start.6
  17.6 0.7 copy-start.8
  18.9 0.7 copy-start.3
  19.6 0.7 copy-start.4
  20.3 0.6 copy-start.7
  31.2 0.8 copy-start.9
  32.0 38.5 %copy-start.2 = (bf16[128,1024]{1,0:T(8,128)(2,1)S(1)}, bf16[128,1024]{1,0:T(8,128)(2,1)}, u32[]{:S(2)}) copy-start(bf16[128,1024]{1,0:T(8,128)(2,1)} %tokens_ref.1) | copy-start | bytes 786436
  70.5 2.5 %copy-start.10 = (f32[1024]{0:T(1024)S(1)}, f32[1024]{0:T(1024)}, u32[]{:S(2)}) copy-start(f32[1024]{0:T(1024)} %param.25) | copy-start | bytes 12292
  70.5 2.5 %copy-start.11 = (f32[1024]{0:T(1024)S(1)}, f32[1024]{0:T(1024)}, u32[]{:S(2)}) copy-start(f32[1024]{0:T(1024)} %param.24) | copy-start | bytes 12292
  73.9 63.5 %reduce-scatter.2.cloned.1.call-start = ((), (), s32[]{:S(2)}) async-start(), calls=%async_computation.4 | async-start | bytes 1310720 | tf_op jit(solution)/shard_map/reduce_scatter | solution.py:313
  110.6 29.3 %copy-start.12 = (f32[1024]{0:T(1024)S(1)}, f32[1024]{0:T(1024)}, u32[]{:S(2)}) copy-start(f32[1024]{0:T(1024)} %param.27) | copy-start | bytes 12292
  110.6 29.3 %copy-start.13 = (f32[1024]{0:T(1024)S(1)}, f32[1024]{0:T(1024)}, u32[]{:S(2)}) copy-start(f32[1024]{0:T(1024)} %param.26) | copy-start | bytes 12292
Sparse Core Ops, SparseCore 0:
  74.0 27.3 all-gather.1
  110.8 26.6 reduce-scatter.1

commit v2 on v1

--- a/solution.py
+++ b/solution.py
@@ -12,6 +12,8 @@
 TILE = 64
 MASKED = -1e30
 VMEM_LIMIT = 56 * 1024 * 1024
+
+ALL = ("req", "other", "pair")
 
 epsilon = 1e-05
 
@@ -106,24 +108,45 @@
     sorted_ref,
     proj_ref,
     att_ref,
+    w_held,
+    keys_held,
+    values_held,
+    sems,
 ):
     slots, width = x_ref.shape
     requests, context, _ = keys_ref.shape
     head_dim = width // HEADS
     span = GROUP * head_dim
     scale = head_dim ** (-0.5)
+    loads = [
+        pltpu.make_async_copy(
+            w_ref.at[:, i * width : (i + 1) * width],
+            w_held.at[:, i * width : (i + 1) * width],
+            sems.at[i],
+        )
+        for i in range(3)
+    ]
+    loads.append(pltpu.make_async_copy(keys_ref, keys_held, sems.at[3]))
+    loads.append(pltpu.make_async_copy(values_ref, values_held, sems.at[4]))
+    for load in loads:
+        load.start()
     sorted_ref[...] = jnp.dot(
         sort_ref[...], x_ref[...], preferred_element_type=jnp.float32
     ).astype(jnp.bfloat16)
     att_ref[...] = jnp.zeros_like(att_ref)
 
-    @pl.loop(0, 3 * width // span)
-    def _(c):
-        columns = pl.ds(pl.multiple_of(c * span, span), span)
-        proj_ref[:, columns] = jnp.dot(
-            sorted_ref[...], w_ref[:, columns], preferred_element_type=jnp.float32
-        ).astype(jnp.bfloat16)
-
+    for i in range(3):
+        loads[i].wait()
+
+        @pl.loop(0, width // span)
+        def _(c):
+            columns = pl.ds(pl.multiple_of(i * width + c * span, span), span)
+            proj_ref[:, columns] = jnp.dot(
+                sorted_ref[...], w_held[:, columns], preferred_element_type=jnp.float32
+            ).astype(jnp.bfloat16)
+
+    loads[3].wait()
+    loads[4].wait()
     starts = [starts_ref[r, 0] for r in range(requests + 1)]
     filled = starts[requests]
 
@@ -158,8 +181,8 @@
                     )
                     k_new = proj_ref[:, width + lo : width + lo + span]
                     v_new = proj_ref[:, 2 * width + lo : 2 * width + lo + span]
-                    k_old = keys_ref[r, :, lo : lo + span]
-                    v_old = values_ref[r, :, lo : lo + span]
+                    k_old = keys_held[r, :, lo : lo + span]
+                    v_old = values_held[r, :, lo : lo + span]
                     across = (((1,), (1,)), ((), ()))
                     s_old = (
                         lax.dot_general(q, k_old, across, preferred_element_type=jnp.float32)
@@ -199,8 +222,70 @@
     ).astype(jnp.bfloat16)
 
 
+def out_kernel(back_ref, returned_ref, w_ref, tokens_ref, gain_ref, shift_ref, out_ref):
+    rows = jnp.dot(
+        back_ref[...], returned_ref[...], preferred_element_type=jnp.float32
+    ).astype(jnp.bfloat16)
+    summed = jnp.dot(rows, w_ref[...], preferred_element_type=jnp.float32)
+    summed = summed + tokens_ref[...].astype(jnp.float32)
+    out_ref[...] = layer_norm(summed, gain_ref[...], shift_ref[...]).astype(jnp.bfloat16)
+
+
+def gelu(hidden):
+    return (0.5 * hidden * (1.0 + lax.erf(hidden * (0.5**0.5)))).astype(jnp.bfloat16)
+
+
+def ffn_part(x, fc1, fc2):
+    hidden = gelu(jnp.dot(x, fc1, preferred_element_type=jnp.float32))
+    return jnp.dot(hidden, fc2, preferred_element_type=jnp.float32)
+
+
+def ffn_kernel(x_ref, fc1_ref, fc2_ref, out_ref):
+    out_ref[...] = ffn_part(x_ref[...], fc1_ref[...], fc2_ref[...])
+
+
+def unpack(pieces, pair_ref, width):
+    pair = pair_ref[...].reshape(pieces, -1, pair_ref.shape[-1])
+    rows = width // pieces
+    hidden = pair.shape[1] * pieces * pair.shape[2] // width - pair.shape[2]
+    return pair[:, :rows].reshape(width, -1), pair[:, rows:].reshape(hidden, width)
+
+
+def own_kernel(pieces, x_ref, base_ref, pair_ref, out_ref):
+    pair = unpack(pieces, pair_ref, x_ref.shape[1])
+    out_ref[...] = base_ref[...] + ffn_part(x_ref[...], *pair)
+
+
+def visitor_kernel(pieces, x_ref, fc1_ref, fc2_ref, pair_ref, out_ref):
+    total = ffn_part(x_ref[...], fc1_ref[...], fc2_ref[...])
+    pair = unpack(pieces, pair_ref, x_ref.shape[1])
+    out_ref[...] = (total + ffn_part(x_ref[...], *pair)).astype(out_ref.dtype)
+
+
+def final_kernel(gain_ref, shift_ref, normed_ref, *refs):
+    summed = normed_ref[...].astype(jnp.float32)
+    for part_ref in refs[:-1]:
+        summed = summed + part_ref[...].astype(jnp.float32)
+    refs[-1][...] = layer_norm(summed, gain_ref[...], shift_ref[...]).astype(jnp.bfloat16)
+
+
+def piece_of(*weights):
+    pieces = lax.axis_size("req")
+    index = lax.axis_index("req")
+    shares = [
+        lax.dynamic_slice_in_dim(w, index * (w.shape[0] // pieces), w.shape[0] // pieces)
+        for w in weights
+    ]
+    columns = min(w.shape[1] for w in weights)
+    return jnp.concatenate([s.reshape(-1, columns) for s in shares], axis=0)
+
+
 def vmem(n):
     return [pl.BlockSpec(memory_space=pltpu.VMEM)] * n
+
+
+def hbm(n):
+    return [pl.BlockSpec(memory_space=pltpu.HBM)] * n
 
 
 def smem(n):
@@ -231,11 +316,10 @@
     ln2_gain,
     ln2_bias,
 ):
-    n_req = lax.axis_size("req")
-    n_mlp = lax.axis_size("mlp")
-    devices = n_req * n_mlp
-    owner_index = lax.axis_index("req") * n_mlp + lax.axis_index("mlp")
+    devices = lax.axis_size(ALL)
+    owner_index = lax.axis_index(ALL)
     tok_dev, width = tokens.shape
+    piece = piece_of(w_fc1, w_fc2)
     capacity = max(2, 2 * tok_dev // devices)
     slots = devices * capacity
     me = owner_index.astype(jnp.int32).reshape(1)
@@ -251,7 +335,7 @@
     )(me, owners, tokens)
     arrived = lax.all_to_all(
         outgoing.reshape(devices, capacity, width),
-        ("req", "mlp"),
+        ALL,
         split_axis=0,
         concat_axis=0,
         tiled=True,
@@ -270,17 +354,28 @@
         cost_estimate=pl.CostEstimate(flops=40_000_000, bytes_accessed=400_000, transcendentals=0),
         name="table",
     )(me, owners, requests)
+    arrived, piece, back, sort, unsort, starts = lax.optimization_barrier(
+        (arrived, piece, back, sort, unsort, starts)
+    )
+    piece = lax.ppermute(piece, "pair", [(0, 1), (1, 0)])
     attended = pl.pallas_call(
         attend_kernel,
         out_shape=shape((slots, width)),
-        in_specs=smem(2) + vmem(6),
+        in_specs=smem(2) + vmem(3) + hbm(3),
         out_specs=vmem(1)[0],
         scratch_shapes=[
             pltpu.VMEM((slots, width), jnp.bfloat16),
             pltpu.VMEM((slots, 3 * width), jnp.bfloat16),
             pltpu.VMEM((slots, width), jnp.bfloat16),
+            pltpu.VMEM(w_qkv.shape, jnp.bfloat16),
+            pltpu.VMEM(cache_k.shape, jnp.bfloat16),
+            pltpu.VMEM(cache_v.shape, jnp.bfloat16),
+            pltpu.SemaphoreType.DMA((5,)),
         ],
         compiler_params=params(),
+        cost_estimate=pl.CostEstimate(
+            flops=16 * slots * width * width, bytes_accessed=20_000_000, transcendentals=4_000_000
+        ),
         name="attend",
     )(
         starts,
@@ -292,50 +387,98 @@
         cache_k,
         cache_v,
     )
+    attended, piece = lax.optimization_barrier((attended, piece))
+    pair = lax.all_gather(piece, "req", axis=0, tiled=True)
     returned = lax.all_to_all(
         attended.reshape(devices, capacity, width),
-        ("req", "mlp"),
+        ALL,
         split_axis=0,
         concat_axis=0,
         tiled=True,
     )
-    attn_rows = jnp.dot(
-        back, returned.reshape(slots, width), preferred_element_type=jnp.float32
-    ).astype(jnp.bfloat16)
-    projected_out = jnp.dot(attn_rows, w_out, preferred_element_type=jnp.float32)
-    normed = layer_norm(projected_out + tokens.astype(jnp.float32), ln1_gain, ln1_bias).astype(
-        jnp.bfloat16
-    )
-    gathered = lax.all_gather(normed, "mlp", axis=0, tiled=True)
-    hidden = jax.nn.gelu(
-        jnp.dot(gathered, w_fc1, preferred_element_type=jnp.float32), approximate=False
-    ).astype(jnp.bfloat16)
-    summed = lax.psum_scatter(
-        jnp.dot(hidden, w_fc2, preferred_element_type=jnp.float32).astype(jnp.bfloat16),
-        "mlp",
-        scatter_dimension=0,
-        tiled=True,
-    ).astype(jnp.float32)
-    return layer_norm(normed.astype(jnp.float32) + summed, ln2_gain, ln2_bias).astype(jnp.bfloat16)
+    normed = pl.pallas_call(
+        out_kernel,
+        out_shape=shape((tok_dev, width)),
+        in_specs=vmem(6),
+        out_specs=vmem(1)[0],
+        compiler_params=params(16 * 1024 * 1024),
+        name="out_norm",
+    )(
+        back,
+        returned.reshape(slots, width),
+        w_out,
+        tokens,
+        ln1_gain.reshape(1, width),
+        ln1_bias.reshape(1, width),
+    )
+    others = lax.axis_size("other")
+    pieces = lax.axis_size("req")
+
+    def ffn_call(name, kernel, operands, dtype, pairs):
+        return pl.pallas_call(
+            kernel,
+            out_shape=shape((tok_dev, width), dtype),
+            in_specs=vmem(len(operands)),
+            out_specs=vmem(1)[0],
+            compiler_params=params(16 * 1024 * 1024),
+            cost_estimate=pl.CostEstimate(
+                flops=4 * tok_dev * w_fc1.size * pairs,
+                bytes_accessed=4 * w_fc1.size * pairs,
+                transcendentals=0,
+            ),
+            name=name,
+        )(*operands)
+
+    def shift(states, by):
+        return lax.ppermute(states, "other", [(i, i ^ by) for i in range(others)])
+
+    visitors = [shift(normed, by) for by in range(1, others)]
+    own = ffn_call("ffn_own", ffn_kernel, (normed, w_fc1, w_fc2), jnp.float32, 1)
+    visitors, own = lax.optimization_barrier((visitors, own))
+    parts = []
+    for by, visitor in enumerate(visitors, 1):
+        part = ffn_call(
+            "ffn_visitor",
+            functools.partial(visitor_kernel, pieces),
+            (visitor, w_fc1, w_fc2, pair),
+            jnp.bfloat16,
+            2,
+        )
+        parts.append(shift(part, by))
+    own = ffn_call(
+        "ffn_pair", functools.partial(own_kernel, pieces), (normed, own, pair), jnp.float32, 1
+    )
+    parts.append(own)
+    return pl.pallas_call(
+        final_kernel,
+        out_shape=shape((tok_dev, width)),
+        in_specs=vmem(len(parts) + 3),
+        out_specs=vmem(1)[0],
+        compiler_params=params(16 * 1024 * 1024),
+        name="final_norm",
+    )(ln2_gain.reshape(1, width), ln2_bias.reshape(1, width), normed, *parts)
 
 
 def solution(mesh):
+    n_req, n_mlp = mesh.devices.shape
+    split = jax.sharding.Mesh(mesh.devices.reshape(n_req, n_mlp // 2, 2), ALL)
+    mlp = ("other", "pair")
     placed = (
-        P(("req", "mlp"), None),
-        P(),
-        P(),
-        P(("req", "mlp")),
-        P(("req", "mlp"), None, None),
-        P(("req", "mlp"), None, None),
-        P(),
-        P(),
-        P(None, "mlp"),
-        P("mlp", None),
+        P(ALL, None),
+        P(),
+        P(),
+        P(ALL),
+        P(ALL, None, None),
+        P(ALL, None, None),
+        P(),
+        P(),
+        P(None, mlp),
+        P(mlp, None),
         P(),
         P(),
         P(),
         P(),
     )
     return jax.shard_map(
-        per_device, mesh=mesh, in_specs=placed, out_specs=P(("req", "mlp"), None), check_vma=False
-    )
+        per_device, mesh=split, in_specs=placed, out_specs=P(ALL, None), check_vma=False
+    )

time: 150 us -> 118 us (0.79)
  waiting for transfers between devices: 64.7 us -> 36.5 us
  matrix products: 11.4 us -> 0 us
  starting transfers between devices: 7.38 us -> 14.2 us
  local copies, waits for them, and re-layouts: 5.96 us -> 12.3 us
  other arithmetic: 5.53 us -> 0.04 us
  Pallas kernels: 21.3 us -> 23.1 us
    reduce_scatter x1 -> x0, waiting for transfers between devices: 26.8 us -> none  [per_device(): lax.psum_scatter(jnp.dot(hidden, w_fc2, preferred_element_type=jnp.float3...]
    all_gather x1, waiting for transfers between devices: 27.5 us -> 2.53 us  [per_device(): pair = lax.all_gather(piece, 'req', axis=0, tiled=True)]
    ppermute x0 -> x3, waiting for transfers between devices: none -> 24.7 us  [the longest x2 24.7 us: shift(): return lax.ppermute(states, 'other', [(i, i ^ by) for i in range(others)])]
    dot_general x2 -> x0, matrix products: 11.4 us -> none  [the longest x1 9.13 us: per_device(): jnp.dot(hidden, w_fc2, preferred_element_type=jnp.float32)]
    ppermute x0 -> x3, starting transfers between devices: none -> 6.91 us  [the longest x2 4.37 us: shift(): return lax.ppermute(states, 'other', [(i, i ^ by) for i in range(others)])]
    unnamed x28 -> x40, local copies, waits for them, and re-layouts: 5.96 us -> 11.2 us
    pallas_call x0 -> x5, Pallas kernels: none -> 4.71 us  [the longest x3 2.94 us: ffn_call(): pl.pallas_call(kernel, out_shape=shape((tok_dev, width), dtype), in_specs...]
    pallas_call x1, Pallas kernels: 19.6 us -> 16.6 us  [per_device(): pl.pallas_call(attend_kernel, out_shape=shape((slots, width)), in_specs=s...]
  transfers between devices with their start and end apart: 3 -> 5, of which waited for: 3 -> 4; matrix products, arithmetic and copies ran while one was open for 0% -> 1% of each run, Pallas kernels for 0% -> 17%
where the time goes in v2:
time: 118 us; the launch traced here: 117 us
  waiting for transfers between devices  36.5 us (31%)
  Pallas kernels  23.1 us (20%)
  blocking collectives  17.5 us (15%)
  starting transfers between devices  14.2 us (12%)
  between operations  13.6 us (12%)
  local copies, waits for them, and re-layouts  12.3 us (10%)
    ppermute x2, waiting for transfers between devices, shift(): return lax.ppermute(states, 'other', [(i, i ^ by) for i in range(others)])  24.7 us
    all_to_all x1, blocking collectives, per_device(): lax.all_to_all(attended.reshape(devices, capacity, width), ALL, split_axi...  17.5 us
    pallas_call x1, Pallas kernels, per_device(): pl.pallas_call(attend_kernel, out_shape=shape((slots, width)), in_specs=s...  16.6 us
    unnamed x40, local copies, waits for them, and re-layouts  11.2 us
    all_to_all x1, waiting for transfers between devices, per_device(): lax.all_to_all(outgoing.reshape(devices, capacity, width), ALL, split_axi...  9.24 us
    all_to_all x1, starting transfers between devices, per_device(): lax.all_to_all(outgoing.reshape(devices, capacity, width), ALL, split_axi...  7.3 us
    ppermute x2, starting transfers between devices, shift(): return lax.ppermute(states, 'other', [(i, i ^ by) for i in range(others)])  4.37 us
    pallas_call x3, Pallas kernels, ffn_call(): pl.pallas_call(kernel, out_shape=shape((tok_dev, width), dtype), in_specs...  2.94 us
  transfers between devices with their start and end apart: 5, of which 4 were waited for; matrix products, arithmetic and copies ran while one was open for 1% of the time, Pallas kernels for 17%

profile of v2, /device:TPU:0, one launch (start us, length us, event | category | flops | bytes accessed | tf_op | source)
XLA Modules:
  0.0 117.2 jit_solution(17919396869203337033)
XLA Ops:
  6.5 0.9 copy-done.6
  7.5 0.7 copy-done.10
  8.2 1.2 %dispatch.1 = bf16[256,1024]{1,0:T(8,128)(2,1)} custom-call(s32[1]{0:T(128)} %bitcast.2.me_ref, s32[32,128]{1,0:T(8,128)S(1)} %bitcast.12, bf16[128,1024]{1,0:T(8,128)(2,1)S(1)} %copy-done.6), custom_call_target="tpu_custom_call" | custom-call | tf_op jit(solution)/shard_map/dispatch/pallas_call | solution.py:328
  9.4 7.3 %all-to-all-start = ((bf16[32,8,1024]{2,1,0:T(8,128)(2,1)}), bf16[32,8,1024]{2,1,0:T(8,128)(2,1)S(1)}, u32[]{:S(2)}, u32[]{:S(2)}) async-start(bf16[32,8,1024]{2,1,0:T(8,128)(2,1)} %bitcast.4), calls=%async_computation | async-start | bytes 1048576 | tf_op jit(solution)/shard_map/all_to_all | solution.py:336
  16.7 0.0 all-gather.2.cloned.1.call-start
  16.7 0.0 copy-start.11
  16.8 0.7 copy-done.11
  17.5 0.7 copy-done.17
  18.2 0.6 table.1
  18.8 0.6 copy-done.8
  19.5 0.7 copy-done.9
  20.1 0.6 copy-done.16
  20.7 1.1 constant_dynamic-slice_fusion
  21.8 9.2 %all-to-all-done = bf16[32,8,1024]{2,1,0:T(8,128)(2,1)S(1)} async-done(((bf16[32,8,1024]{2,1,0:T(8,128)(2,1)}), bf16[32,8,1024]{2,1,0:T(8,128)(2,1)S(1)}, u32[]{:S(2)}, u32[]{:S(2)}) %all-to-all-start) | async-done | bytes 524320 | tf_op jit(solution)/shard_map/all_to_all | solution.py:336
  31.1 2.5 %collective-permute-start = (bf16[256,1024]{1,0:T(8,128)(2,1)S(1)}, bf16[256,1024]{1,0:T(8,128)(2,1)S(1)}, u32[]{:S(2)}, u32[]{:S(2)}) collective-permute-start(bf16[256,1024]{1,0:T(8,128)(2,1)S(1)} %pad_maximum_fusion), channel_id=1, source_target_pairs={{0,1},{1,0},{2,3},{3,2},{4,5},{5,4},{6,7},{7,6},{8,9},{9,8},{10,11... | collective-permute-start | bytes 1572872 | tf_op jit(solution)/shard_map/ppermute | solution.py:360
  33.6 16.6 %attend.1 = bf16[256,1024]{1,0:T(8,128)(2,1)} custom-call(s32[8,128]{1,0:T(8,128)} %copy-done.16, s32[4]{0:T(128)} %lengths_ref.1, bf16[256,256]{1,0:T(8,128)(2,1)} %copy-done.8, bf16[256,256]{1,0:T(8,128)(2,1)} %copy-done.9, bf16[256,1024]{1,0:T(8,128)(2,1)} %bitcast.19, bf16[1024,3072]{1,0:T(8,128)(2,1)} %w_ref.2, bf16[4,512,1024]{2,1,0:T(8,128)(2,1)} %keys_ref.1, ...), custom_call_target="tpu_custom_call" | custom-call | flops 4294967296 | bytes 20000000 | tf_op jit(solution)/shard_map/attend/pallas_call | solution.py:361
  50.3 0.8 copy-done.19
  51.1 0.0 all-gather.2.cloned.1.call-update
  51.1 17.5 %all_to_all.10 = bf16[32,8,1024]{2,1,0:T(8,128)(2,1)S(1)} all-to-all(bf16[32,8,1024]{2,1,0:T(8,128)(2,1)} %bitcast.20), channel_id=1, replica_groups=mesh['req'=8,'other'=2,'pair'=2] {'req','other','pair'}, dimensions={0} | all-to-all | bytes 1048576 | tf_op jit(solution)/shard_map/all_to_all | solution.py:392
  68.6 1.6 %copy-done.5 = bf16[1024,1024]{1,0:T(8,128)(2,1)S(1)} copy-done((bf16[1024,1024]{1,0:T(8,128)(2,1)S(1)}, bf16[1024,1024]{1,0:T(8,128)(2,1)}, u32[]{:S(2)}) %copy-start.5) | copy-done | bytes 2097176
  70.2 0.8 out_norm.1.x_ref.normed_ref
  71.0 1.9 %collective-permute-start.1 = (bf16[128,1024]{1,0:T(8,128)(2,1)S(1)}, bf16[128,1024]{1,0:T(8,128)(2,1)S(1)}, u32[]{:S(2)}, u32[]{:S(2)}) collective-permute-start(bf16[128,1024]{1,0:T(8,128)(2,1)S(1)} %out_norm.1.x_ref.normed_ref), channel_id=1, source_target_pairs={{0,2},{2,0},{1,3},{3,1},{4,6},{6,4},{5,7},{7,5},{8,10},{10,8},{9,1... | collective-permute-start | bytes 786440 | tf_op jit(solution)/shard_map/ppermute | solution.py:433
  72.9 0.8 ffn_own.1.base_ref
  73.7 12.9 %collective-permute-done.1.x_ref = bf16[128,1024]{1,0:T(8,128)(2,1)S(1)} collective-permute-done((bf16[128,1024]{1,0:T(8,128)(2,1)S(1)}, bf16[128,1024]{1,0:T(8,128)(2,1)S(1)}, u32[]{:S(2)}, u32[]{:S(2)}) %collective-permute-start.1) | collective-permute-done | bytes 262176 | tf_op jit(solution)/shard_map/ppermute | solution.py:433
  86.6 2.5 %all-gather.2.cloned.1.call-done.pair_ref = bf16[2048,1024]{1,0:T(8,128)(2,1)} async-done(((bf16[256,1024]{1,0:T(8,128)(2,1)}), bf16[2048,1024]{1,0:T(8,128)(2,1)}) %all-gather.2.cloned.1.call-update) | async-done | bytes 4194320 | tf_op jit(solution)/shard_map/all_gather | solution.py:391
  89.2 2.2 %copy-done = bf16[2048,1024]{1,0:T(8,128)(2,1)S(1)} copy-done((bf16[2048,1024]{1,0:T(8,128)(2,1)S(1)}, bf16[2048,1024]{1,0:T(8,128)(2,1)}, u32[]{:S(2)}) %copy-start) | copy-done | bytes 4194328
  91.4 1.6 %copy-done.4 = bf16[1024,1024]{1,0:T(8,128)(2,1)S(1)} copy-done((bf16[1024,1024]{1,0:T(8,128)(2,1)S(1)}, bf16[1024,1024]{1,0:T(8,128)(2,1)}, u32[]{:S(2)}) %copy-start.4) | copy-done | bytes 2097176
  93.0 1.4 %ffn_visitor.1 = bf16[128,1024]{1,0:T(8,128)(2,1)S(1)} custom-call(bf16[128,1024]{1,0:T(8,128)(2,1)S(1)} %collective-permute-done.1.x_ref, bf16[1024,1024]{1,0:T(8,128)(2,1)S(1)} %copy-done.2, bf16[1024,1024]{1,0:T(8,128)(2,1)S(1)} %copy-done.4, bf16[2048,1024]{1,0:T(8,128)(2,1)S(1)} %copy-done), custom_call_target="tpu_custom_call" | custom-call | flops 1073741824 | bytes 8388608 | tf_op jit(solution)/shard_map/ffn_visitor/pallas_call | solution.py:418
  94.4 2.5 %collective-permute-start.2 = (bf16[128,1024]{1,0:T(8,128)(2,1)S(1)}, bf16[128,1024]{1,0:T(8,128)(2,1)S(1)}, u32[]{:S(2)}, u32[]{:S(2)}) collective-permute-start(bf16[128,1024]{1,0:T(8,128)(2,1)S(1)} %ffn_visitor.1), channel_id=1, source_target_pairs={{0,2},{2,0},{1,3},{3,1},{4,6},{6,4},{5,7},{7,5},{8,10},{10,8},{9,1... | collective-permute-start | bytes 786440 | tf_op jit(solution)/shard_map/ppermute | solution.py:433
  96.8 0.8 ffn_pair.1.refs_1_
  97.6 11.8 %collective-permute-done.2.refs_0_ = bf16[128,1024]{1,0:T(8,128)(2,1)S(1)} collective-permute-done((bf16[128,1024]{1,0:T(8,128)(2,1)S(1)}, bf16[128,1024]{1,0:T(8,128)(2,1)S(1)}, u32[]{:S(2)}, u32[]{:S(2)}) %collective-permute-start.2) | collective-permute-done | bytes 262176 | tf_op jit(solution)/shard_map/ppermute | solution.py:433
  109.4 1.0 final_norm.1
  (30 shorter events, 0.1 us)
Async XLA Ops:
  6.5 0.9 copy-start.6
  7.5 0.7 copy-start.10
  9.4 21.7 %all-to-all-start = ((bf16[32,8,1024]{2,1,0:T(8,128)(2,1)}), bf16[32,8,1024]{2,1,0:T(8,128)(2,1)S(1)}, u32[]{:S(2)}, u32[]{:S(2)}) async-start(bf16[32,8,1024]{2,1,0:T(8,128)(2,1)} %bitcast.4), calls=%async_computation | async-start | bytes 1048576 | tf_op jit(solution)/shard_map/all_to_all | solution.py:336
  16.7 72.5 %all-gather.2.cloned.1.call-start = ((), (), s32[]{:S(2)}) async-start(), calls=%async_computation.2 | async-start | bytes 4718592 | tf_op jit(solution)/shard_map/all_gather | solution.py:391
  16.7 0.7 copy-start.11
  17.5 0.7 copy-start.17
  18.8 0.7 copy-start.8
  19.5 0.7 copy-start.9
  20.1 0.6 copy-start.16
  31.1 2.5 %copy-start.18 = (bf16[32,8,1024]{2,1,0:T(8,128)(2,1)}, bf16[32,8,1024]{2,1,0:T(8,128)(2,1)S(1)}, u32[]{:S(2)}) copy-start(bf16[32,8,1024]{2,1,0:T(8,128)(2,1)S(1)} %all-to-all-done) | copy-start | bytes 1572868
  31.1 19.2 %collective-permute-start = (bf16[256,1024]{1,0:T(8,128)(2,1)S(1)}, bf16[256,1024]{1,0:T(8,128)(2,1)S(1)}, u32[]{:S(2)}, u32[]{:S(2)}) collective-permute-start(bf16[256,1024]{1,0:T(8,128)(2,1)S(1)} %pad_maximum_fusion), channel_id=1, source_target_pairs={{0,1},{1,0},{2,3},{3,2},{4,5},{5,4},{6,7},{7,6},{8,9},{9,8},{10,11... | collective-permute-start | bytes 1572872 | tf_op jit(solution)/shard_map/ppermute | solution.py:360
  33.6 35.0 %copy-start.7 = (bf16[128,1024]{1,0:T(8,128)(2,1)S(1)}, bf16[128,1024]{1,0:T(8,128)(2,1)}, u32[]{:S(2)}) copy-start(bf16[128,1024]{1,0:T(8,128)(2,1)} %tokens_ref.3) | copy-start | bytes 786436
  33.6 35.0 %copy-start.12 = (f32[1024]{0:T(1024)S(1)}, f32[1024]{0:T(1024)}, u32[]{:S(2)}) copy-start(f32[1024]{0:T(1024)} %param.24) | copy-start | bytes 12292
  33.6 35.0 %copy-start.13 = (f32[1024]{0:T(1024)S(1)}, f32[1024]{0:T(1024)}, u32[]{:S(2)}) copy-start(f32[1024]{0:T(1024)} %param.25) | copy-start | bytes 12292
  50.3 0.8 copy-start.19
  51.1 21.8 %copy-start.2 = (bf16[1024,1024]{1,0:T(8,128)(2,1)S(1)}, bf16[1024,1024]{1,0:T(8,128)(2,1)}, u32[]{:S(2)}) copy-start(bf16[1024,1024]{1,0:T(8,128)(2,1)} %fc1_ref.3) | copy-start | bytes 6291460
  51.1 21.8 %copy-start.3 = (bf16[1024,1024]{1,0:T(8,128)(2,1)S(1)}, bf16[1024,1024]{1,0:T(8,128)(2,1)}, u32[]{:S(2)}) copy-start(bf16[1024,1024]{1,0:T(8,128)(2,1)} %fc2_ref.3) | copy-start | bytes 6291460
  68.6 1.6 %copy-start.5 = (bf16[1024,1024]{1,0:T(8,128)(2,1)S(1)}, bf16[1024,1024]{1,0:T(8,128)(2,1)}, u32[]{:S(2)}) copy-start(bf16[1024,1024]{1,0:T(8,128)(2,1)} %w_ref.3) | copy-start | bytes 6291460
  71.0 15.6 %collective-permute-start.1 = (bf16[128,1024]{1,0:T(8,128)(2,1)S(1)}, bf16[128,1024]{1,0:T(8,128)(2,1)S(1)}, u32[]{:S(2)}, u32[]{:S(2)}) collective-permute-start(bf16[128,1024]{1,0:T(8,128)(2,1)S(1)} %out_norm.1.x_ref.normed_ref), channel_id=1, source_target_pairs={{0,2},{2,0},{1,3},{3,1},{4,6},{6,4},{5,7},{7,5},{8,10},{10,8},{9,1... | collective-permute-start | bytes 786440 | tf_op jit(solution)/shard_map/ppermute | solution.py:433
  89.2 2.2 %copy-start = (bf16[2048,1024]{1,0:T(8,128)(2,1)S(1)}, bf16[2048,1024]{1,0:T(8,128)(2,1)}, u32[]{:S(2)}) copy-start(bf16[2048,1024]{1,0:T(8,128)(2,1)} %all-gather.2.cloned.1.call-done.pair_ref) | copy-start | bytes 12582916
  91.4 1.6 %copy-start.4 = (bf16[1024,1024]{1,0:T(8,128)(2,1)S(1)}, bf16[1024,1024]{1,0:T(8,128)(2,1)}, u32[]{:S(2)}) copy-start(bf16[1024,1024]{1,0:T(8,128)(2,1)} %fc2_ref.3) | copy-start | bytes 6291460
  93.0 3.9 %copy-start.1 = (bf16[2048,1024]{1,0:T(8,128)(2,1)S(1)}, bf16[2048,1024]{1,0:T(8,128)(2,1)}, u32[]{:S(2)}) copy-start(bf16[2048,1024]{1,0:T(8,128)(2,1)} %all-gather.2.cloned.1.call-done.pair_ref) | copy-start | bytes 12582916
  94.3 15.1 %copy-start.14 = (f32[1024]{0:T(1024)S(1)}, f32[1024]{0:T(1024)}, u32[]{:S(2)}) copy-start(f32[1024]{0:T(1024)} %param.26) | copy-start | bytes 12292
  94.3 15.1 %copy-start.15 = (f32[1024]{0:T(1024)S(1)}, f32[1024]{0:T(1024)}, u32[]{:S(2)}) copy-start(f32[1024]{0:T(1024)} %param.27) | copy-start | bytes 12292
  94.4 15.1 %collective-permute-start.2 = (bf16[128,1024]{1,0:T(8,128)(2,1)S(1)}, bf16[128,1024]{1,0:T(8,128)(2,1)S(1)}, u32[]{:S(2)}, u32[]{:S(2)}) collective-permute-start(bf16[128,1024]{1,0:T(8,128)(2,1)S(1)} %ffn_visitor.1), channel_id=1, source_target_pairs={{0,2},{2,0},{1,3},{3,1},{4,6},{6,4},{5,7},{7,5},{8,10},{10,8},{9,1... | collective-permute-start | bytes 786440 | tf_op jit(solution)/shard_map/ppermute | solution.py:433
Sparse Core Ops, SparseCore 0:
  51.2 37.9 all-gather.1

commit v3 on v2

--- a/solution.py
+++ b/solution.py
@@ -9,7 +9,7 @@
 
 HEADS = 16
 GROUP = 4
-TILE = 64
+TILE = 80
 MASKED = -1e30
 VMEM_LIMIT = 56 * 1024 * 1024
 
@@ -34,8 +34,15 @@
     return across, across.T
 
 
-def dispatch_kernel(capacity, me_ref, owners_ref, tokens_ref, out_ref):
+def dispatch_kernel(capacity, me_ref, owners_hbm, tokens_hbm, out_ref, owners_ref, tokens_ref, sems):
+    loads = [
+        pltpu.make_async_copy(owners_hbm, owners_ref, sems.at[0]),
+        pltpu.make_async_copy(tokens_hbm, tokens_ref, sems.at[1]),
+    ]
+    for load in loads:
+        load.start()
     tok_dev = tokens_ref.shape[0]
+    loads[0].wait()
     slots = out_ref.shape[0]
     across, down = own_pairs(owners_ref, me_ref[0])
     square = (tok_dev, tok_dev)
@@ -44,6 +51,7 @@
     column = across[:1, :] * capacity + rank
     onehot = iota((slots, tok_dev), 0).astype(jnp.float32) == column
     onehot = jnp.where(onehot, 1.0, 0.0).astype(jnp.bfloat16)
+    loads[1].wait()
     out_ref[...] = jnp.dot(
         onehot, tokens_ref[...], preferred_element_type=jnp.float32
     ).astype(jnp.bfloat16)
@@ -111,111 +119,126 @@
     w_held,
     keys_held,
     values_held,
-    sems,
+    w_sems,
+    cache_sems,
 ):
     slots, width = x_ref.shape
     requests, context, _ = keys_ref.shape
     head_dim = width // HEADS
     span = GROUP * head_dim
+    groups = width // span
     scale = head_dim ** (-0.5)
-    loads = [
-        pltpu.make_async_copy(
-            w_ref.at[:, i * width : (i + 1) * width],
-            w_held.at[:, i * width : (i + 1) * width],
-            sems.at[i],
+
+    def w_load(part):
+        columns = pl.ds(part * width, width)
+        return pltpu.make_async_copy(
+            w_ref.at[:, columns], w_held.at[:, columns], w_sems.at[part]
         )
-        for i in range(3)
-    ]
-    loads.append(pltpu.make_async_copy(keys_ref, keys_held, sems.at[3]))
-    loads.append(pltpu.make_async_copy(values_ref, values_held, sems.at[4]))
-    for load in loads:
-        load.start()
+
+    def cache_load(r, ref, held, i):
+        return pltpu.make_async_copy(ref.at[r], held.at[r], cache_sems.at[r, i])
+
+    def start_cache(r):
+        cache_load(r, keys_ref, keys_held, 0).start()
+        cache_load(r, values_ref, values_held, 1).start()
+
+    ahead = min(2, requests)
+    for part in range(3):
+        w_load(part).start()
     sorted_ref[...] = jnp.dot(
         sort_ref[...], x_ref[...], preferred_element_type=jnp.float32
     ).astype(jnp.bfloat16)
     att_ref[...] = jnp.zeros_like(att_ref)
-
-    for i in range(3):
-        loads[i].wait()
-
-        @pl.loop(0, width // span)
-        def _(c):
-            columns = pl.ds(pl.multiple_of(i * width + c * span, span), span)
-            proj_ref[:, columns] = jnp.dot(
+    for part in range(3):
+        w_load(part).wait()
+        if 0 < part <= ahead:
+            start_cache(part - 1)
+
+        for c in range(2):
+            columns = pl.ds(part * width + c * (width // 2), width // 2)
+            projected = jnp.dot(
                 sorted_ref[...], w_held[:, columns], preferred_element_type=jnp.float32
             ).astype(jnp.bfloat16)
-
-    loads[3].wait()
-    loads[4].wait()
-    starts = [starts_ref[r, 0] for r in range(requests + 1)]
-    filled = starts[requests]
-
-    @pl.loop(0, pl.cdiv(filled, TILE))
-    def _(t):
-        first = pl.multiple_of(t * TILE, TILE)
+            proj_ref[:, columns] = projected
+
+    row_step = 16
+    window = min(slots, 128)
+    head_of = iota((1, span), 1) // head_dim
+    across = (((1,), (1,)), ((), ()))
+
+    def attend(r, first, begin, end, length, old, new, new_first):
         rows = pl.ds(first, TILE)
-        last = jnp.minimum(first + TILE, filled) - 1
-        low = sum((starts[r] <= first).astype(jnp.int32) for r in range(1, requests))
-        high = sum((starts[r] <= last).astype(jnp.int32) for r in range(1, requests))
-
-        @pl.loop(low, high + 1)
-        def _(r):
-            begin, end = starts_ref[r, 0], starts_ref[r + 1, 0]
-
-            @pl.when(end > begin)
-            def _():
-                row = iota((TILE, 1), 0) + first
-                in_request = (row >= begin) & (row < end)
-                key = iota((1, slots), 1)
-                seen = (key >= begin) & (key <= row)
-                new_bias = jnp.where(seen, 0.0, MASKED)
-                new_bias = jnp.concatenate([new_bias] * GROUP, axis=0)
-                valid = iota((1, context), 1) < lengths_ref[r]
-                old_bias = jnp.where(valid, 0.0, MASKED)
-                head_of = iota((1, span), 1) // head_dim
-                for g in range(HEADS // GROUP):
-                    lo = g * span
-                    q = proj_ref[rows, lo : lo + span]
-                    q = jnp.concatenate(
-                        [jnp.where(head_of == h, q, jnp.bfloat16(0)) for h in range(GROUP)], axis=0
-                    )
-                    k_new = proj_ref[:, width + lo : width + lo + span]
-                    v_new = proj_ref[:, 2 * width + lo : 2 * width + lo + span]
-                    k_old = keys_held[r, :, lo : lo + span]
-                    v_old = values_held[r, :, lo : lo + span]
-                    across = (((1,), (1,)), ((), ()))
-                    s_old = (
-                        lax.dot_general(q, k_old, across, preferred_element_type=jnp.float32)
-                        * scale
-                        + old_bias
-                    )
-                    s_new = (
-                        lax.dot_general(q, k_new, across, preferred_element_type=jnp.float32)
-                        * scale
-                        + new_bias
-                    )
-                    top = jnp.maximum(
-                        jnp.max(s_old, axis=1, keepdims=True), jnp.max(s_new, axis=1, keepdims=True)
-                    )
-                    p_old = jnp.exp(s_old - top)
-                    p_new = jnp.exp(s_new - top)
-                    total = jnp.sum(p_old, axis=1, keepdims=True) + jnp.sum(
-                        p_new, axis=1, keepdims=True
-                    )
-                    part = jnp.dot(
-                        p_old.astype(jnp.bfloat16), v_old, preferred_element_type=jnp.float32
-                    )
-                    part += jnp.dot(
-                        p_new.astype(jnp.bfloat16), v_new, preferred_element_type=jnp.float32
-                    )
-                    part = part / total
-                    mixed = jnp.zeros((TILE, span), jnp.float32)
-                    for h in range(GROUP):
-                        mixed = jnp.where(head_of == h, part[h * TILE : (h + 1) * TILE], mixed)
-                    kept = att_ref[rows, lo : lo + span]
-                    att_ref[rows, lo : lo + span] = jnp.where(
-                        in_request, mixed.astype(jnp.bfloat16), kept
-                    )
+        fresh = pl.ds(new_first, new)
+        row = iota((TILE, 1), 0) + first
+        key = iota((1, new), 1) + new_first
+        new_bias = jnp.where((key >= begin) & (key <= row), 0.0, MASKED)
+        new_bias = jnp.concatenate([new_bias] * GROUP, axis=0)
+        old_bias = jnp.where(iota((1, old), 1) < length, 0.0, MASKED)
+        mixes = []
+        for g in range(groups):
+            lo = g * span
+            q = proj_ref[rows, lo : lo + span]
+            q = jnp.concatenate(
+                [jnp.where(head_of == h, q, jnp.bfloat16(0)) for h in range(GROUP)], axis=0
+            )
+            k_new = proj_ref[fresh, width + lo : width + lo + span]
+            v_new = proj_ref[fresh, 2 * width + lo : 2 * width + lo + span]
+            k_old = keys_held[r, :old, lo : lo + span]
+            v_old = values_held[r, :old, lo : lo + span]
+            s_old = (
+                lax.dot_general(q, k_old, across, preferred_element_type=jnp.float32) * scale
+                + old_bias
+            )
+            s_new = (
+                lax.dot_general(q, k_new, across, preferred_element_type=jnp.float32) * scale
+                + new_bias
+            )
+            top = jnp.maximum(
+                jnp.max(s_old, axis=1, keepdims=True), jnp.max(s_new, axis=1, keepdims=True)
+            )
+            p_old = jnp.exp(s_old - top)
+            p_new = jnp.exp(s_new - top)
+            total = jnp.sum(p_old, axis=1, keepdims=True) + jnp.sum(p_new, axis=1, keepdims=True)
+            part = jnp.dot(
+                jnp.concatenate([p_old.astype(jnp.bfloat16), p_new.astype(jnp.bfloat16)], axis=1),
+                jnp.concatenate([v_old, v_new], axis=0),
+                preferred_element_type=jnp.float32,
+            )
+            part = part * (1.0 / total)
+            mixed = part[:TILE]
+            for h in range(1, GROUP):
+                mixed = jnp.where(head_of == h, part[h * TILE : (h + 1) * TILE], mixed)
+            mixes.append(mixed.astype(jnp.bfloat16))
+        inside = (row >= begin) & (row < end)
+        att_ref[rows, :] = jnp.where(inside, jnp.concatenate(mixes, axis=1), att_ref[rows, :])
+
+    @pl.loop(0, requests)
+    def _(r):
+        cache_load(r, keys_ref, keys_held, 0).wait()
+        cache_load(r, values_ref, values_held, 1).wait()
+
+        @pl.when(r + ahead < requests)
+        def _():
+            start_cache(r + ahead)
+
+        begin, end = starts_ref[r, 0], starts_ref[r + 1, 0]
+        length = lengths_ref[r]
+        base = begin // row_step * row_step
+
+        @pl.loop(0, jnp.where(end > begin, pl.cdiv(end - base, TILE), 0))
+        def _(t):
+            first = pl.multiple_of(jnp.minimum(base + t * TILE, slots - TILE), row_step)
+            new_first = pl.multiple_of(jnp.minimum(base, slots - window), row_step)
+            few_new = end <= new_first + window
+            few_old = length <= context // 2
+
+            for old, is_old in ((context // 2, few_old), (context, ~few_old)):
+                for new, is_new in ((window, few_new), (slots, ~few_new)):
+
+                    @pl.when(is_old & is_new)
+                    def _():
+                        start = new_first if new < slots else 0
+                        attend(r, first, begin, end, length, old, new, start)
 
     out_ref[...] = jnp.dot(
         unsort_ref[...], att_ref[...], preferred_element_type=jnp.float32
@@ -244,22 +267,15 @@
     out_ref[...] = ffn_part(x_ref[...], fc1_ref[...], fc2_ref[...])
 
 
-def unpack(pieces, pair_ref, width):
-    pair = pair_ref[...].reshape(pieces, -1, pair_ref.shape[-1])
+def pair_kernel(x_ref, base_ref, pair_ref, out_ref):
+    pieces = pair_ref.shape[0]
+    width = x_ref.shape[1]
     rows = width // pieces
-    hidden = pair.shape[1] * pieces * pair.shape[2] // width - pair.shape[2]
-    return pair[:, :rows].reshape(width, -1), pair[:, rows:].reshape(hidden, width)
-
-
-def own_kernel(pieces, x_ref, base_ref, pair_ref, out_ref):
-    pair = unpack(pieces, pair_ref, x_ref.shape[1])
-    out_ref[...] = base_ref[...] + ffn_part(x_ref[...], *pair)
-
-
-def visitor_kernel(pieces, x_ref, fc1_ref, fc2_ref, pair_ref, out_ref):
-    total = ffn_part(x_ref[...], fc1_ref[...], fc2_ref[...])
-    pair = unpack(pieces, pair_ref, x_ref.shape[1])
-    out_ref[...] = (total + ffn_part(x_ref[...], *pair)).astype(out_ref.dtype)
+    fc1 = pair_ref[:, :rows].reshape(width, -1)
+    hidden = gelu(jnp.dot(x_ref[...], fc1, preferred_element_type=jnp.float32))
+    fc2 = pair_ref[:, rows:].reshape(fc1.shape[1], width)
+    part = jnp.dot(hidden, fc2, preferred_element_type=jnp.float32)
+    out_ref[...] = (base_ref[...] + part).astype(out_ref.dtype)
 
 
 def final_kernel(gain_ref, shift_ref, normed_ref, *refs):
@@ -328,9 +344,14 @@
     outgoing = pl.pallas_call(
         functools.partial(dispatch_kernel, capacity),
         out_shape=shape((slots, width)),
-        in_specs=smem(1) + vmem(2),
+        in_specs=smem(1) + hbm(2),
         out_specs=vmem(1)[0],
-        compiler_params=params(16 * 1024 * 1024),
+        scratch_shapes=[
+            pltpu.VMEM(owners.shape, owners.dtype),
+            pltpu.VMEM(tokens.shape, tokens.dtype),
+            pltpu.SemaphoreType.DMA((2,)),
+        ],
+        compiler_params=params(),
         name="dispatch",
     )(me, owners, tokens)
     arrived = lax.all_to_all(
@@ -370,9 +391,10 @@
             pltpu.VMEM(w_qkv.shape, jnp.bfloat16),
             pltpu.VMEM(cache_k.shape, jnp.bfloat16),
             pltpu.VMEM(cache_v.shape, jnp.bfloat16),
-            pltpu.SemaphoreType.DMA((5,)),
+            pltpu.SemaphoreType.DMA((3,)),
+            pltpu.SemaphoreType.DMA((cache_k.shape[0], 2)),
         ],
-        compiler_params=params(),
+        compiler_params=params(50 * 1024 * 1024),
         cost_estimate=pl.CostEstimate(
             flops=16 * slots * width * width, bytes_accessed=20_000_000, transcendentals=4_000_000
         ),
@@ -413,42 +435,46 @@
     )
     others = lax.axis_size("other")
     pieces = lax.axis_size("req")
-
-    def ffn_call(name, kernel, operands, dtype, pairs):
+    pair = pair.reshape(pieces, -1, pair.shape[1])
+    cost = pl.CostEstimate(
+        flops=4 * tok_dev * w_fc1.size, bytes_accessed=4 * w_fc1.size, transcendentals=0
+    )
+
+    def near_part(states):
         return pl.pallas_call(
-            kernel,
-            out_shape=shape((tok_dev, width), dtype),
-            in_specs=vmem(len(operands)),
+            ffn_kernel,
+            out_shape=shape((tok_dev, width), jnp.float32),
+            in_specs=vmem(3),
             out_specs=vmem(1)[0],
             compiler_params=params(16 * 1024 * 1024),
-            cost_estimate=pl.CostEstimate(
-                flops=4 * tok_dev * w_fc1.size * pairs,
-                bytes_accessed=4 * w_fc1.size * pairs,
-                transcendentals=0,
-            ),
-            name=name,
-        )(*operands)
+            cost_estimate=cost,
+            name="ffn_near",
+        )(states, w_fc1, w_fc2)
+
+    def pair_part(states, base, dtype):
+        return pl.pallas_call(
+            pair_kernel,
+            out_shape=shape((tok_dev, width), dtype),
+            in_specs=vmem(3),
+            out_specs=vmem(1)[0],
+            compiler_params=params(16 * 1024 * 1024),
+            cost_estimate=cost,
+            name="ffn_pair",
+        )(states, base, pair)
 
     def shift(states, by):
         return lax.ppermute(states, "other", [(i, i ^ by) for i in range(others)])
 
     visitors = [shift(normed, by) for by in range(1, others)]
-    own = ffn_call("ffn_own", ffn_kernel, (normed, w_fc1, w_fc2), jnp.float32, 1)
+    own = near_part(normed)
     visitors, own = lax.optimization_barrier((visitors, own))
-    parts = []
-    for by, visitor in enumerate(visitors, 1):
-        part = ffn_call(
-            "ffn_visitor",
-            functools.partial(visitor_kernel, pieces),
-            (visitor, w_fc1, w_fc2, pair),
-            jnp.bfloat16,
-            2,
-        )
-        parts.append(shift(part, by))
-    own = ffn_call(
-        "ffn_pair", functools.partial(own_kernel, pieces), (normed, own, pair), jnp.float32, 1
-    )
-    parts.append(own)
+    bases = [near_part(visitor) for visitor in visitors]
+    bases, pair = lax.optimization_barrier((bases, pair))
+    parts = [
+        shift(pair_part(visitor, base, jnp.bfloat16), by)
+        for by, (visitor, base) in enumerate(zip(visitors, bases), 1)
+    ]
+    parts.append(pair_part(normed, own, jnp.float32))
     return pl.pallas_call(
         final_kernel,
         out_shape=shape((tok_dev, width)),

time: 118 us -> 109 us (0.924)
  local copies, waits for them, and re-layouts: 12.3 us -> 5.68 us
  Pallas kernels: 23.1 us -> 18.6 us
  waiting for transfers between devices: 36.5 us -> 39.3 us
    unnamed x40 -> x26, local copies, waits for them, and re-layouts: 11.2 us -> 4.61 us
    pallas_call x1, Pallas kernels: 16.6 us -> 10.9 us  [per_device(): pl.pallas_call(attend_kernel, out_shape=shape((slots, width)), in_specs=s...]
    ppermute x1, waiting for transfers between devices: 0.01 us -> 1.89 us  [per_device(): piece = lax.ppermute(piece, 'pair', [(0, 1), (1, 0)])]
    pallas_call x3 -> x4, Pallas kernels: 2.94 us -> 3.22 us  [the longest x2 1.63 us: pair_part(): pl.pallas_call(pair_kernel, out_shape=shape((tok_dev, width), dtype), in_...]
  transfers between devices with their start and end apart: 5 -> 5, of which waited for: 4 -> 5; matrix products, arithmetic and copies ran while one was open for 1% -> 2% of each run, Pallas kernels for 17% -> 14%
where the time goes in v3:
time: 109 us
  waiting for transfers between devices  39.3 us (36%)
  Pallas kernels  18.6 us (17%)
  blocking collectives  16.5 us (15%)
  starting transfers between devices  14.3 us (13%)
  between operations  13.5 us (12%)
  local copies, waits for them, and re-layouts  5.68 us (5%)
    ppermute x2, waiting for transfers between devices, shift(): return lax.ppermute(states, 'other', [(i, i ^ by) for i in range(others)])  24.7 us
    all_to_all x1, blocking collectives, per_device(): lax.all_to_all(attended.reshape(devices, capacity, width), ALL, split_axi...  16.5 us
    pallas_call x1, Pallas kernels, per_device(): pl.pallas_call(attend_kernel, out_shape=shape((slots, width)), in_specs=s...  10.9 us
    all_to_all x1, waiting for transfers between devices, per_device(): lax.all_to_all(outgoing.reshape(devices, capacity, width), ALL, split_axi...  10.3 us
    all_to_all x1, starting transfers between devices, per_device(): lax.all_to_all(outgoing.reshape(devices, capacity, width), ALL, split_axi...  7.3 us
    unnamed x26, local copies, waits for them, and re-layouts  4.61 us
    ppermute x2, starting transfers between devices, shift(): return lax.ppermute(states, 'other', [(i, i ^ by) for i in range(others)])  4.38 us
    ppermute x1, starting transfers between devices, per_device(): piece = lax.ppermute(piece, 'pair', [(0, 1), (1, 0)])  2.54 us
  transfers between devices with their start and end apart: 5, of which 5 were waited for; matrix products, arithmetic and copies ran while one was open for 2% of the time, Pallas kernels for 14%

profile of v3, /device:TPU:0, one launch (start us, length us, event | category | flops | bytes accessed | tf_op | source)
XLA Modules:
  0.0 108.7 jit_solution(13153840367440989711)
XLA Ops:
  6.5 2.1 %dispatch.1 = bf16[256,1024]{1,0:T(8,128)(2,1)} custom-call(s32[1]{0:T(128)} %bitcast.2.me_ref, s32[32,128]{1,0:T(8,128)} %bitcast.17, bf16[128,1024]{1,0:T(8,128)(2,1)} %tokens_ref.1), custom_call_target="tpu_custom_call" | custom-call | tf_op jit(solution)/shard_map/dispatch/pallas_call | solution.py:344
  8.6 7.3 %all-to-all-start = ((bf16[32,8,1024]{2,1,0:T(8,128)(2,1)}), bf16[32,8,1024]{2,1,0:T(8,128)(2,1)S(1)}, u32[]{:S(2)}, u32[]{:S(2)}) async-start(bf16[32,8,1024]{2,1,0:T(8,128)(2,1)} %bitcast.24), calls=%async_computation | async-start | bytes 1048576 | tf_op jit(solution)/shard_map/all_to_all | solution.py:357
  15.9 0.0 all-gather.2.cloned.1.call-start
  16.0 0.0 copy-start.6
  16.0 0.7 copy-done.6
  16.7 0.7 copy-done.12
  17.4 0.6 table.1
  18.1 1.1 constant_dynamic-slice_fusion
  19.1 0.8 pad_maximum_fusion
  20.0 10.3 %all-to-all-done = bf16[32,8,1024]{2,1,0:T(8,128)(2,1)S(1)} async-done(((bf16[32,8,1024]{2,1,0:T(8,128)(2,1)}), bf16[32,8,1024]{2,1,0:T(8,128)(2,1)S(1)}, u32[]{:S(2)}, u32[]{:S(2)}) %all-to-all-start) | async-done | bytes 524320 | tf_op jit(solution)/shard_map/all_to_all | solution.py:357
  30.3 2.5 %collective-permute-start = (bf16[256,1024]{1,0:T(8,128)(2,1)}, bf16[256,1024]{1,0:T(8,128)(2,1)}, u32[]{:S(2)}, u32[]{:S(2)}) collective-permute-start(bf16[256,1024]{1,0:T(8,128)(2,1)} %pad_maximum_fusion), channel_id=1, source_target_pairs={{0,1},{1,0},{2,3},{3,2},{4,5},{5,4},{6,7},{7,6},{8,9},{9,8},{10,11... | collective-permute-start | bytes 1572872 | tf_op jit(solution)/shard_map/ppermute | solution.py:381
  32.9 10.9 %attend.1 = bf16[256,1024]{1,0:T(8,128)(2,1)S(1)} custom-call(s32[8,128]{1,0:T(8,128)S(1)} %get-tuple-element.26.starts_ref, s32[4]{0:T(128)S(1)} %copy-done.11, bf16[256,256]{1,0:T(8,128)(2,1)S(1)} %get-tuple-element.27.sort_ref, bf16[256,256]{1,0:T(8,128)(2,1)S(1)} %get-tuple-element.28.unsort_ref, bf16[256,1024]{1,0:T(8,128)(2,1)S(1)} %bitcast.15, ...), custom_call_target="tpu_custom_call" | custom-call | flops 4294967296 | bytes 20000000 | tf_op jit(solution)/shard_map/attend/pallas_call | solution.py:382
  43.7 1.9 %collective-permute-done = bf16[256,1024]{1,0:T(8,128)(2,1)} collective-permute-done((bf16[256,1024]{1,0:T(8,128)(2,1)}, bf16[256,1024]{1,0:T(8,128)(2,1)}, u32[]{:S(2)}, u32[]{:S(2)}) %collective-permute-start) | collective-permute-done | bytes 524320 | tf_op jit(solution)/shard_map/ppermute | solution.py:381
  45.6 0.0 all-gather.2.cloned.1.call-update
  45.7 0.0 copy-start.2
  45.7 0.0 copy-start.3
  45.7 16.5 %all_to_all.10 = bf16[32,8,1024]{2,1,0:T(8,128)(2,1)S(1)} all-to-all(bf16[32,8,1024]{2,1,0:T(8,128)(2,1)S(1)} %bitcast.16), channel_id=1, replica_groups=mesh['req'=8,'other'=2,'pair'=2] {'req','other','pair'}, dimensions={0} | all-to-all | bytes 1048576 | tf_op jit(solution)/shard_map/all_to_all | solution.py:414
  62.2 0.0 copy-start.5
  62.2 0.9 copy-done.5
  63.2 0.8 out_norm.1.x_ref.normed_ref
  64.0 1.9 %collective-permute-start.1 = (bf16[128,1024]{1,0:T(8,128)(2,1)S(1)}, bf16[128,1024]{1,0:T(8,128)(2,1)S(1)}, u32[]{:S(2)}, u32[]{:S(2)}) collective-permute-start(bf16[128,1024]{1,0:T(8,128)(2,1)S(1)} %out_norm.1.x_ref.normed_ref), channel_id=1, source_target_pairs={{0,2},{2,0},{1,3},{3,1},{4,6},{6,4},{5,7},{7,5},{8,10},{10,8},{9,1... | collective-permute-start | bytes 786440 | tf_op jit(solution)/shard_map/ppermute | solution.py:466
  65.9 0.8 ffn_near.2.base_ref
  66.7 12.9 %collective-permute-done.1.x_ref = bf16[128,1024]{1,0:T(8,128)(2,1)S(1)} collective-permute-done((bf16[128,1024]{1,0:T(8,128)(2,1)S(1)}, bf16[128,1024]{1,0:T(8,128)(2,1)S(1)}, u32[]{:S(2)}, u32[]{:S(2)}) %collective-permute-start.1) | collective-permute-done | bytes 262176 | tf_op jit(solution)/shard_map/ppermute | solution.py:466
  79.6 0.8 ffn_near.3.base_ref
  80.4 2.4 %all-gather.2.cloned.1.call-done = bf16[2048,1024]{1,0:T(8,128)(2,1)} async-done(((bf16[256,1024]{1,0:T(8,128)(2,1)}), bf16[2048,1024]{1,0:T(8,128)(2,1)}) %all-gather.2.cloned.1.call-update) | async-done | bytes 4194320 | tf_op jit(solution)/shard_map/all_gather | solution.py:413
  82.8 2.2 %copy-done = bf16[2048,1024]{1,0:T(8,128)(2,1)S(1)} copy-done((bf16[2048,1024]{1,0:T(8,128)(2,1)S(1)}, bf16[2048,1024]{1,0:T(8,128)(2,1)}, u32[]{:S(2)}) %copy-start) | copy-done | bytes 4194328
  85.0 0.8 ffn_pair.2
  85.8 0.0 copy-start.9
  85.9 2.5 %collective-permute-start.2 = (bf16[128,1024]{1,0:T(8,128)(2,1)S(1)}, bf16[128,1024]{1,0:T(8,128)(2,1)S(1)}, u32[]{:S(2)}, u32[]{:S(2)}) collective-permute-start(bf16[128,1024]{1,0:T(8,128)(2,1)S(1)} %ffn_pair.2), channel_id=1, source_target_pairs={{0,2},{2,0},{1,3},{3,1},{4,6},{6,4},{5,7},{7,5},{8,10},{10,8},{9,1... | collective-permute-start | bytes 786440 | tf_op jit(solution)/shard_map/ppermute | solution.py:466
  88.3 0.8 ffn_pair.3.refs_1_
  89.2 11.8 %collective-permute-done.2.refs_0_ = bf16[128,1024]{1,0:T(8,128)(2,1)S(1)} collective-permute-done((bf16[128,1024]{1,0:T(8,128)(2,1)S(1)}, bf16[128,1024]{1,0:T(8,128)(2,1)S(1)}, u32[]{:S(2)}, u32[]{:S(2)}) %collective-permute-start.2) | collective-permute-done | bytes 262176 | tf_op jit(solution)/shard_map/ppermute | solution.py:466
  100.9 1.0 final_norm.1
  (17 shorter events, 0.0 us)
Async XLA Ops:
  6.5 26.3 %copy-start.11 = (s32[4]{0:T(128)S(1)}, s32[4]{0:T(128)}, u32[]{:S(2)}) copy-start(s32[4]{0:T(128)} %lengths_ref.1) | copy-start | bytes 52
  8.6 21.7 %all-to-all-start = ((bf16[32,8,1024]{2,1,0:T(8,128)(2,1)}), bf16[32,8,1024]{2,1,0:T(8,128)(2,1)S(1)}, u32[]{:S(2)}, u32[]{:S(2)}) async-start(bf16[32,8,1024]{2,1,0:T(8,128)(2,1)} %bitcast.24), calls=%async_computation | async-start | bytes 1048576 | tf_op jit(solution)/shard_map/all_to_all | solution.py:357
  15.9 66.9 %all-gather.2.cloned.1.call-start = ((), (), s32[]{:S(2)}) async-start(), calls=%async_computation.2 | async-start | bytes 4718592 | tf_op jit(solution)/shard_map/all_gather | solution.py:413
  16.0 0.7 copy-start.6
  16.7 0.7 copy-start.12
  30.3 15.3 %collective-permute-start = (bf16[256,1024]{1,0:T(8,128)(2,1)}, bf16[256,1024]{1,0:T(8,128)(2,1)}, u32[]{:S(2)}, u32[]{:S(2)}) collective-permute-start(bf16[256,1024]{1,0:T(8,128)(2,1)} %pad_maximum_fusion), channel_id=1, source_target_pairs={{0,1},{1,0},{2,3},{3,2},{4,5},{5,4},{6,7},{7,6},{8,9},{9,8},{10,11... | collective-permute-start | bytes 1572872 | tf_op jit(solution)/shard_map/ppermute | solution.py:381
  32.9 29.3 %copy-start.4 = (bf16[1024,1024]{1,0:T(8,128)(2,1)S(1)}, bf16[1024,1024]{1,0:T(8,128)(2,1)}, u32[]{:S(2)}) copy-start(bf16[1024,1024]{1,0:T(8,128)(2,1)} %w_ref.3) | copy-start | bytes 6291460
  32.9 29.3 %copy-start.7 = (f32[1024]{0:T(1024)S(1)}, f32[1024]{0:T(1024)}, u32[]{:S(2)}) copy-start(f32[1024]{0:T(1024)} %param.24) | copy-start | bytes 12292
  32.9 29.3 %copy-start.8 = (f32[1024]{0:T(1024)S(1)}, f32[1024]{0:T(1024)}, u32[]{:S(2)}) copy-start(f32[1024]{0:T(1024)} %param.25) | copy-start | bytes 12292
  45.7 20.2 %copy-start.2 = (bf16[1024,1024]{1,0:T(8,128)(2,1)S(1)}, bf16[1024,1024]{1,0:T(8,128)(2,1)}, u32[]{:S(2)}) copy-start(bf16[1024,1024]{1,0:T(8,128)(2,1)} %fc1_ref.3) | copy-start | bytes 6291460
  45.7 20.2 %copy-start.3 = (bf16[1024,1024]{1,0:T(8,128)(2,1)S(1)}, bf16[1024,1024]{1,0:T(8,128)(2,1)}, u32[]{:S(2)}) copy-start(bf16[1024,1024]{1,0:T(8,128)(2,1)} %fc2_ref.3) | copy-start | bytes 6291460
  62.2 1.0 copy-start.5
  64.0 15.6 %collective-permute-start.1 = (bf16[128,1024]{1,0:T(8,128)(2,1)S(1)}, bf16[128,1024]{1,0:T(8,128)(2,1)S(1)}, u32[]{:S(2)}, u32[]{:S(2)}) collective-permute-start(bf16[128,1024]{1,0:T(8,128)(2,1)S(1)} %out_norm.1.x_ref.normed_ref), channel_id=1, source_target_pairs={{0,2},{2,0},{1,3},{3,1},{4,6},{6,4},{5,7},{7,5},{8,10},{10,8},{9,1... | collective-permute-start | bytes 786440 | tf_op jit(solution)/shard_map/ppermute | solution.py:466
  82.8 2.2 %copy-start = (bf16[2048,1024]{1,0:T(8,128)(2,1)S(1)}, bf16[2048,1024]{1,0:T(8,128)(2,1)}, u32[]{:S(2)}) copy-start(bf16[2048,1024]{1,0:T(8,128)(2,1)} %all-gather.2.cloned.1.call-done) | copy-start | bytes 12582916
  85.0 3.3 %copy-start.1 = (bf16[2048,1024]{1,0:T(8,128)(2,1)S(1)}, bf16[2048,1024]{1,0:T(8,128)(2,1)}, u32[]{:S(2)}) copy-start(bf16[2048,1024]{1,0:T(8,128)(2,1)} %all-gather.2.cloned.1.call-done) | copy-start | bytes 12582916
  85.8 15.1 %copy-start.9 = (f32[1024]{0:T(1024)S(1)}, f32[1024]{0:T(1024)}, u32[]{:S(2)}) copy-start(f32[1024]{0:T(1024)} %param.26) | copy-start | bytes 12292
  85.9 15.1 %copy-start.10 = (f32[1024]{0:T(1024)S(1)}, f32[1024]{0:T(1024)}, u32[]{:S(2)}) copy-start(f32[1024]{0:T(1024)} %param.27) | copy-start | bytes 12292
  85.9 15.0 %collective-permute-start.2 = (bf16[128,1024]{1,0:T(8,128)(2,1)S(1)}, bf16[128,1024]{1,0:T(8,128)(2,1)S(1)}, u32[]{:S(2)}, u32[]{:S(2)}) collective-permute-start(bf16[128,1024]{1,0:T(8,128)(2,1)S(1)} %ffn_pair.2), channel_id=1, source_target_pairs={{0,2},{2,0},{1,3},{3,1},{4,6},{6,4},{5,7},{7,5},{8,10},{10,8},{9,1... | collective-permute-start | bytes 786440 | tf_op jit(solution)/shard_map/ppermute | solution.py:466
Sparse Core Ops, SparseCore 0:
  45.8 37.0 all-gather.1

commit v4 on v3

--- a/solution.py
+++ b/solution.py
@@ -278,10 +278,35 @@
     out_ref[...] = (base_ref[...] + part).astype(out_ref.dtype)
 
 
-def final_kernel(gain_ref, shift_ref, normed_ref, *refs):
-    summed = normed_ref[...].astype(jnp.float32)
-    for part_ref in refs[:-1]:
-        summed = summed + part_ref[...].astype(jnp.float32)
+def assemble_kernel(me_ref, *refs):
+    pieces, (fc1_ref, fc2_ref, sems) = refs[:-3], refs[-3:]
+    rows = fc1_ref.shape[0] // len(pieces)
+    copies = []
+    for k, piece in enumerate(pieces):
+        place = pl.ds(pl.multiple_of((me_ref[0] ^ k) * rows, rows), rows)
+        for i, out_ref in enumerate((fc1_ref, fc2_ref)):
+            copies.append(
+                pltpu.make_async_copy(
+                    piece.at[i * rows : (i + 1) * rows], out_ref.at[place], sems.at[i, k]
+                )
+            )
+    for copy in copies:
+        copy.start()
+    for copy in copies:
+        copy.wait()
+
+
+def whole_kernel(x_ref, fc1_ref, fc2_ref, pair_fc1_ref, pair_fc2_ref, out_ref):
+    total = ffn_part(x_ref[...], fc1_ref[...], fc2_ref[...])
+    total += ffn_part(x_ref[...], pair_fc1_ref[...], pair_fc2_ref[...])
+    out_ref[...] = total.astype(out_ref.dtype)
+
+
+def final_kernel(halves, gain_ref, shift_ref, normed_ref, own_ref, *refs):
+    summed = normed_ref[...].astype(jnp.float32) + own_ref[...]
+    for i in range(0, len(refs) - 1, halves):
+        part = jnp.concatenate([ref[...] for ref in refs[i : i + halves]], axis=0)
+        summed = summed + part.astype(jnp.float32)
     refs[-1][...] = layer_norm(summed, gain_ref[...], shift_ref[...]).astype(jnp.bfloat16)
 
 
@@ -410,7 +435,18 @@
         cache_v,
     )
     attended, piece = lax.optimization_barrier((attended, piece))
-    pair = lax.all_gather(piece, "req", axis=0, tiled=True)
+    sharers = lax.axis_size("req")
+    rows = w_fc1.shape[0] // sharers
+    by_permutes = rows % 128 == 0 and w_fc1.shape[0] == w_fc1.shape[1]
+
+    def from_sharer(piece, by):
+        return lax.ppermute(piece, "req", [(i, i ^ by) for i in range(sharers)])
+
+    if by_permutes:
+        mate = from_sharer(piece, 1)
+        shares = [from_sharer(piece, by) for by in range(2, sharers, 2)]
+    else:
+        pair = lax.all_gather(piece, "req", axis=0, tiled=True)
     returned = lax.all_to_all(
         attended.reshape(devices, capacity, width),
         ALL,
@@ -434,8 +470,6 @@
         ln1_bias.reshape(1, width),
     )
     others = lax.axis_size("other")
-    pieces = lax.axis_size("req")
-    pair = pair.reshape(pieces, -1, pair.shape[1])
     cost = pl.CostEstimate(
         flops=4 * tok_dev * w_fc1.size, bytes_accessed=4 * w_fc1.size, transcendentals=0
     )
@@ -465,24 +499,63 @@
     def shift(states, by):
         return lax.ppermute(states, "other", [(i, i ^ by) for i in range(others)])
 
-    visitors = [shift(normed, by) for by in range(1, others)]
-    own = near_part(normed)
-    visitors, own = lax.optimization_barrier((visitors, own))
-    bases = [near_part(visitor) for visitor in visitors]
-    bases, pair = lax.optimization_barrier((bases, pair))
-    parts = [
-        shift(pair_part(visitor, base, jnp.bfloat16), by)
-        for by, (visitor, base) in enumerate(zip(visitors, bases), 1)
-    ]
-    parts.append(pair_part(normed, own, jnp.float32))
+    if by_permutes:
+        halves = 2
+        half = tok_dev // halves
+        visitors = [
+            [shift(normed[i * half : (i + 1) * half], by) for i in range(halves)]
+            for by in range(1, others)
+        ]
+        shares, visitors[0][0] = lax.optimization_barrier((shares, visitors[0][0]))
+        shares = [piece, mate] + [got for s in shares for got in (s, from_sharer(s, 1))]
+        me_req = lax.axis_index("req").astype(jnp.int32).reshape(1)
+        pair_weights = pl.pallas_call(
+            assemble_kernel,
+            out_shape=(shape(w_fc1.shape), shape(w_fc2.shape)),
+            in_specs=smem(1) + vmem(len(shares)),
+            out_specs=tuple(vmem(2)),
+            scratch_shapes=[pltpu.SemaphoreType.DMA((2, len(shares)))],
+            compiler_params=params(16 * 1024 * 1024),
+            cost_estimate=cost,
+            name="assemble",
+        )(me_req, *shares)
+
+        def whole(states, dtype):
+            return pl.pallas_call(
+                whole_kernel,
+                out_shape=shape(states.shape, dtype),
+                in_specs=vmem(5),
+                out_specs=vmem(1)[0],
+                compiler_params=params(16 * 1024 * 1024),
+                cost_estimate=cost,
+                name="ffn_whole",
+            )(states, w_fc1, w_fc2, *pair_weights)
+
+        parts = []
+        for by, pair_visitors in enumerate(visitors, 1):
+            parts += [shift(whole(visitor, jnp.bfloat16), by) for visitor in pair_visitors]
+        own = whole(normed, jnp.float32)
+    else:
+        halves = 1
+        pair = pair.reshape(sharers, -1, pair.shape[1])
+        visitors = [shift(normed, by) for by in range(1, others)]
+        own = near_part(normed)
+        visitors, own = lax.optimization_barrier((visitors, own))
+        bases = [near_part(visitor) for visitor in visitors]
+        bases, pair = lax.optimization_barrier((bases, pair))
+        parts = [
+            shift(pair_part(visitor, base, jnp.bfloat16), by)
+            for by, (visitor, base) in enumerate(zip(visitors, bases), 1)
+        ]
+        own = pair_part(normed, own, jnp.float32)
     return pl.pallas_call(
-        final_kernel,
+        functools.partial(final_kernel, halves),
         out_shape=shape((tok_dev, width)),
-        in_specs=vmem(len(parts) + 3),
+        in_specs=vmem(len(parts) + 4),
         out_specs=vmem(1)[0],
         compiler_params=params(16 * 1024 * 1024),
         name="final_norm",
-    )(ln2_gain.reshape(1, width), ln2_bias.reshape(1, width), normed, *parts)
+    )(ln2_gain.reshape(1, width), ln2_bias.reshape(1, width), normed, own, *parts)
 
 
 def solution(mesh):

time: 109 us -> 98.3 us (0.902)
  blocking collectives: 16.5 us -> 0 us
  between operations: 13.5 us -> 0.2 us
  starting transfers between devices: 14.3 us -> 25.3 us
  Pallas kernels: 18.6 us -> 23.1 us
  waiting for transfers between devices: 39.3 us -> 43.6 us
    all_to_all x1 -> x0, blocking collectives: 16.5 us -> none  [per_device(): lax.all_to_all(attended.reshape(devices, capacity, width), ALL, split_axi...]
    ppermute x2 -> x4, waiting for transfers between devices: 24.7 us -> 8.87 us  [shift(): return lax.ppermute(states, 'other', [(i, i ^ by) for i in range(others)])]
    ppermute x0 -> x7, waiting for transfers between devices: none -> 13.8 us  [from_sharer(): return lax.ppermute(piece, 'req', [(i, i ^ by) for i in range(sharers)])]
    all_to_all x0 -> x1, waiting for transfers between devices: none -> 10.6 us  [per_device(): lax.all_to_all(attended.reshape(devices, capacity, width), ALL, split_axi...]
    ppermute x0 -> x7, starting transfers between devices: none -> 4.66 us  [from_sharer(): return lax.ppermute(piece, 'req', [(i, i ^ by) for i in range(sharers)])]
    all_to_all x0 -> x1, starting transfers between devices: none -> 3.54 us  [per_device(): lax.all_to_all(attended.reshape(devices, capacity, width), ALL, split_axi...]
    pallas_call x5, Pallas kernels: 4.2 us -> 7.53 us  [the longest x3 4.56 us: whole(): pl.pallas_call(whole_kernel, out_shape=shape(states.shape, dtype), in_spe...]
    ppermute x2 -> x4, starting transfers between devices: 4.38 us -> 7.29 us  [shift(): return lax.ppermute(states, 'other', [(i, i ^ by) for i in range(others)])]
  transfers between devices with their start and end apart: 5 -> 14, of which waited for: 5 -> 7; matrix products, arithmetic and copies ran while one was open for 2% -> 2% of each run, Pallas kernels for 14% -> 20%
where the time goes in v4:
time: 98.3 us; the launch traced here: 98.1 us
  waiting for transfers between devices  43.6 us (44%)
  starting transfers between devices  25.3 us (26%)
  Pallas kernels  23.1 us (23%)
  local copies, waits for them, and re-layouts  5.07 us (5%)
    ppermute x7, waiting for transfers between devices, from_sharer(): return lax.ppermute(piece, 'req', [(i, i ^ by) for i in range(sharers)])  13.8 us
    pallas_call x1, Pallas kernels, per_device(): pl.pallas_call(attend_kernel, out_shape=shape((slots, width)), in_specs=s...  12.1 us
    all_to_all x1, waiting for transfers between devices, per_device(): lax.all_to_all(attended.reshape(devices, capacity, width), ALL, split_axi...  10.6 us
    all_to_all x1, waiting for transfers between devices, per_device(): lax.all_to_all(outgoing.reshape(devices, capacity, width), ALL, split_axi...  10.3 us
    ppermute x4, waiting for transfers between devices, shift(): return lax.ppermute(states, 'other', [(i, i ^ by) for i in range(others)])  8.87 us
    all_to_all x1, starting transfers between devices, per_device(): lax.all_to_all(outgoing.reshape(devices, capacity, width), ALL, split_axi...  7.31 us
    ppermute x4, starting transfers between devices, shift(): return lax.ppermute(states, 'other', [(i, i ^ by) for i in range(others)])  7.29 us
    ppermute x7, starting transfers between devices, from_sharer(): return lax.ppermute(piece, 'req', [(i, i ^ by) for i in range(sharers)])  4.66 us
  transfers between devices with their start and end apart: 14, of which 7 were waited for; matrix products, arithmetic and copies ran while one was open for 2% of the time, Pallas kernels for 20%

profile of v4, /device:TPU:0, one launch (start us, length us, event | category | flops | bytes accessed | tf_op | source)
XLA Modules:
  0.0 98.1 jit_solution(13346958729736229508)
XLA Ops:
  0.0 2.1 %dispatch.1 = bf16[256,1024]{1,0:T(8,128)(2,1)} custom-call(s32[1]{0:T(128)} %bitcast.2.me_ref, s32[32,128]{1,0:T(8,128)} %bitcast.14, bf16[128,1024]{1,0:T(8,128)(2,1)} %tokens_ref.1), custom_call_target="tpu_custom_call" | custom-call | tf_op jit(solution)/shard_map/dispatch/pallas_call | solution.py:369
  2.1 7.3 %all-to-all-start = ((bf16[32,8,1024]{2,1,0:T(8,128)(2,1)}), bf16[32,8,1024]{2,1,0:T(8,128)(2,1)S(1)}, u32[]{:S(2)}, u32[]{:S(2)}) async-start(bf16[32,8,1024]{2,1,0:T(8,128)(2,1)} %bitcast.21), calls=%async_computation | async-start | bytes 1048576 | tf_op jit(solution)/shard_map/all_to_all | solution.py:382
  9.4 0.7 copy-done.8
  10.1 0.7 copy-done.14
  10.8 0.6 table.1
  11.5 1.1 %constant_dynamic-slice_fusion = (bf16[128,1024]{1,0:T(8,128)(2,1)S(1)}, bf16[128,1024]{1,0:T(8,128)(2,1)S(1)}) fusion(bf16[1024,1024]{1,0:T(8,128)(2,1)} %fc2_ref.5, s32[]{:T(128)S(6)} %select_n.4, bf16[1024,1024]{1,0:T(8,128)(2,1)} %fc1_ref.5), kind=kLoop, calls=%fused_computation.1 | loop fusion | bytes 1048580 | tf_op jit(solution)/shard_map/dynamic_slice | solution.py:317
  12.6 0.8 pad_maximum_fusion
  13.5 10.3 %all-to-all-done = bf16[32,8,1024]{2,1,0:T(8,128)(2,1)S(1)} async-done(((bf16[32,8,1024]{2,1,0:T(8,128)(2,1)}), bf16[32,8,1024]{2,1,0:T(8,128)(2,1)S(1)}, u32[]{:S(2)}, u32[]{:S(2)}) %all-to-all-start) | async-done | bytes 524320 | tf_op jit(solution)/shard_map/all_to_all | solution.py:382
  23.8 2.5 %collective-permute-start = (bf16[256,1024]{1,0:T(8,128)(2,1)}, bf16[256,1024]{1,0:T(8,128)(2,1)S(1)}, u32[]{:S(2)}, u32[]{:S(2)}) collective-permute-start(bf16[256,1024]{1,0:T(8,128)(2,1)} %pad_maximum_fusion), channel_id=1, source_target_pairs={{0,1},{1,0},{2,3},{3,2},{4,5},{5,4},{6,7},{7,6},{8,9},{9,8},{10,11... | collective-permute-start | bytes 1572872 | tf_op jit(solution)/shard_map/ppermute | solution.py:406
  26.3 0.9 copy-done.5
  27.2 12.1 %attend.1 = bf16[256,1024]{1,0:T(8,128)(2,1)} custom-call(s32[8,128]{1,0:T(8,128)S(1)} %get-tuple-element.28.starts_ref, s32[4]{0:T(128)S(1)} %copy-done.13, bf16[256,256]{1,0:T(8,128)(2,1)S(1)} %get-tuple-element.29.sort_ref, bf16[256,256]{1,0:T(8,128)(2,1)S(1)} %copy-done.5, bf16[256,1024]{1,0:T(8,128)(2,1)S(1)} %bitcast.13, bf16[1024,3072]{1,0:T(8,128)(2,1)} %w_ref.2, ...), custom_call_target="tpu_custom_call" | custom-call | flops 4294967296 | bytes 20000000 | tf_op jit(solution)/shard_map/attend/pallas_call | solution.py:407
  39.3 3.5 %all-to-all-start.1 = ((bf16[32,8,1024]{2,1,0:T(8,128)(2,1)}), bf16[32,8,1024]{2,1,0:T(8,128)(2,1)S(1)}, u32[]{:S(2)}, u32[]{:S(2)}) async-start(bf16[32,8,1024]{2,1,0:T(8,128)(2,1)} %bitcast.7), calls=%async_computation.1 | async-start | bytes 1048576 | tf_op jit(solution)/shard_map/all_to_all | solution.py:450
  42.9 2.6 %collective-permute-start.4 = (bf16[256,1024]{1,0:T(8,128)(2,1)S(1)}, bf16[256,1024]{1,0:T(8,128)(2,1)}, u32[]{:S(2)}, u32[]{:S(2)}) collective-permute-start(bf16[256,1024]{1,0:T(8,128)(2,1)S(1)} %collective-permute-done.refs_0_), channel_id=1, source_target_pairs={{0,24},{4,28},{8,16},{12,20},{16,8},{20,12},{24,0},{28,4},{1,25},{... | collective-permute-start | bytes 1572872 | tf_op jit(solution)/shard_map/ppermute | solution.py:443
  45.4 0.6 collective-permute-start.3
  46.4 10.6 %all-to-all-done.1 = bf16[32,8,1024]{2,1,0:T(8,128)(2,1)S(1)} async-done(((bf16[32,8,1024]{2,1,0:T(8,128)(2,1)}), bf16[32,8,1024]{2,1,0:T(8,128)(2,1)S(1)}, u32[]{:S(2)}, u32[]{:S(2)}) %all-to-all-start.1) | async-done | bytes 524320 | tf_op jit(solution)/shard_map/all_to_all | solution.py:450
  57.1 0.8 copy-done.7
  57.9 0.8 out_norm.1.x_ref.normed_ref
  58.8 1.9 %collective-permute-start.5 = (bf16[64,1024]{1,0:T(8,128)(2,1)S(1)}, bf16[64,1024]{1,0:T(8,128)(2,1)S(1)}, u32[]{:S(2)}, u32[]{:S(2)}) collective-permute-start(bf16[64,1024]{1,0:T(8,128)(2,1)S(1)} %get-tuple-element.42), channel_id=1, source_target_pairs={{0,2},{2,0},{1,3},{3,1},{4,6},{6,4},{5,7},{7,5},{8,10},{10,8},{9,1... | collective-permute-start | bytes 393224 | tf_op jit(solution)/shard_map/ppermute | solution.py:500
  61.2 3.0 %collective-permute-done.4.refs_6_ = bf16[256,1024]{1,0:T(8,128)(2,1)} collective-permute-done((bf16[256,1024]{1,0:T(8,128)(2,1)S(1)}, bf16[256,1024]{1,0:T(8,128)(2,1)}, u32[]{:S(2)}, u32[]{:S(2)}) %collective-permute-start.4) | collective-permute-done | bytes 524320 | tf_op jit(solution)/shard_map/ppermute | solution.py:443
  64.2 10.1 %collective-permute-done.3.refs_4_ = bf16[256,1024]{1,0:T(8,128)(2,1)} collective-permute-done((bf16[256,1024]{1,0:T(8,128)(2,1)S(1)}, bf16[256,1024]{1,0:T(8,128)(2,1)}, u32[]{:S(2)}, u32[]{:S(2)}) %collective-permute-start.3) | collective-permute-done | bytes 524320 | tf_op jit(solution)/shard_map/ppermute | solution.py:443
  74.9 2.3 %collective-permute-start.10 = (bf16[64,1024]{1,0:T(8,128)(2,1)S(1)}, bf16[64,1024]{1,0:T(8,128)(2,1)S(1)}, u32[]{:S(2)}, u32[]{:S(2)}) collective-permute-start(bf16[64,1024]{1,0:T(8,128)(2,1)S(1)} %get-tuple-element.41), channel_id=1, source_target_pairs={{0,2},{2,0},{1,3},{3,1},{4,6},{6,4},{5,7},{7,5},{8,10},{10,8},{9,1... | collective-permute-start | bytes 393224 | tf_op jit(solution)/shard_map/ppermute | solution.py:500
  77.2 0.7 collective-permute-done.8.refs_7_
  77.9 2.0 %assemble.1 = (bf16[1024,1024]{1,0:T(8,128)(2,1)S(1)}, bf16[1024,1024]{1,0:T(8,128)(2,1)S(1)}) custom-call(s32[1]{0:T(128)} %bitcast.11.me_ref, bf16[256,1024]{1,0:T(8,128)(2,1)S(1)} %collective-permute-done.refs_0_, bf16[256,1024]{1,0:T(8,128)(2,1)S(1)} %collective-permute-done.1.refs_1_, bf16[256,1024]{1,0:T(8,128)(2,1)} %collective-permute-done.2.refs_2_, ...), custom_call_target="tpu_custom_call" | custom-call | flops 536870912 | bytes 4194304 | tf_op jit(solution)/shard_map/assemble/pallas_call | solution.py:512
  80.0 0.6 copy-done.1
  80.6 1.6 %ffn_whole.4 = bf16[64,1024]{1,0:T(8,128)(2,1)S(1)} custom-call(bf16[64,1024]{1,0:T(8,128)(2,1)S(1)} %collective-permute-done.5.x_ref, bf16[1024,1024]{1,0:T(8,128)(2,1)S(1)} %copy-done, bf16[1024,1024]{1,0:T(8,128)(2,1)S(1)} %copy-done.1, bf16[1024,1024]{1,0:T(8,128)(2,1)S(1)} %get-tuple-element.38.pair_fc1_ref, ...), custom_call_target="tpu_custom_call" | custom-call | flops 536870912 | bytes 4194304 | tf_op jit(solution)/shard_map/ffn_whole/pallas_call | solution.py:524
  82.2 2.4 %collective-permute-start.9 = (bf16[64,1024]{1,0:T(8,128)(2,1)S(1)}, bf16[64,1024]{1,0:T(8,128)(2,1)S(1)}, u32[]{:S(2)}, u32[]{:S(2)}) collective-permute-start(bf16[64,1024]{1,0:T(8,128)(2,1)S(1)} %ffn_whole.4), channel_id=1, source_target_pairs={{0,2},{2,0},{1,3},{3,1},{4,6},{6,4},{5,7},{7,5},{8,10},{10,8},{9,1... | collective-permute-start | bytes 393224 | tf_op jit(solution)/shard_map/ppermute | solution.py:500
  84.6 1.6 %ffn_whole.5 = bf16[64,1024]{1,0:T(8,128)(2,1)S(1)} custom-call(bf16[64,1024]{1,0:T(8,128)(2,1)S(1)} %collective-permute-done.10.x_ref, bf16[1024,1024]{1,0:T(8,128)(2,1)S(1)} %copy-done, bf16[1024,1024]{1,0:T(8,128)(2,1)S(1)} %copy-done.1, bf16[1024,1024]{1,0:T(8,128)(2,1)S(1)} %get-tuple-element.38.pair_fc1_ref, ...), custom_call_target="tpu_custom_call" | custom-call | flops 536870912 | bytes 4194304 | tf_op jit(solution)/shard_map/ffn_whole/pallas_call | solution.py:524
  86.3 0.6 collective-permute-start.11
  86.9 1.4 %ffn_whole.3.own_ref = f32[128,1024]{1,0:T(8,128)S(1)} custom-call(bf16[128,1024]{1,0:T(8,128)(2,1)S(1)} %out_norm.1.x_ref.normed_ref, bf16[1024,1024]{1,0:T(8,128)(2,1)S(1)} %copy-done, bf16[1024,1024]{1,0:T(8,128)(2,1)S(1)} %copy-done.1, bf16[1024,1024]{1,0:T(8,128)(2,1)S(1)} %get-tuple-element.38.pair_fc1_ref, ...), custom_call_target="tpu_custom_call" | custom-call | flops 536870912 | bytes 4194304 | tf_op jit(solution)/shard_map/ffn_whole/pallas_call | solution.py:524
  88.3 6.9 %collective-permute-done.9.refs_0_ = bf16[64,1024]{1,0:T(8,128)(2,1)S(1)} collective-permute-done((bf16[64,1024]{1,0:T(8,128)(2,1)S(1)}, bf16[64,1024]{1,0:T(8,128)(2,1)S(1)}, u32[]{:S(2)}, u32[]{:S(2)}) %collective-permute-start.9) | collective-permute-done | bytes 131104 | tf_op jit(solution)/shard_map/ppermute | solution.py:500
  95.2 2.0 %collective-permute-done.11.refs_1_ = bf16[64,1024]{1,0:T(8,128)(2,1)S(1)} collective-permute-done((bf16[64,1024]{1,0:T(8,128)(2,1)S(1)}, bf16[64,1024]{1,0:T(8,128)(2,1)S(1)}, u32[]{:S(2)}, u32[]{:S(2)}) %collective-permute-start.11) | collective-permute-done | bytes 131104 | tf_op jit(solution)/shard_map/ppermute | solution.py:500
  97.2 1.0 %final_norm.1 = bf16[128,1024]{1,0:T(8,128)(2,1)} custom-call(f32[1,1024]{1,0:T(1,128)S(1)} %bitcast.18, f32[1,1024]{1,0:T(1,128)S(1)} %bitcast.19, bf16[128,1024]{1,0:T(8,128)(2,1)S(1)} %out_norm.1.x_ref.normed_ref, f32[128,1024]{1,0:T(8,128)S(1)} %ffn_whole.3.own_ref, bf16[64,1024]{1,0:T(8,128)(2,1)S(1)} %collective-permute-done.9.refs_0_, ...), custom_call_target="tpu_custom_call" | custom-call | tf_op jit(solution)/shard_map/final_norm/pallas_call | solution.py:551
  (38 shorter events, 1.7 us)
Async XLA Ops:
  0.0 26.3 %copy-start.13 = (s32[4]{0:T(128)S(1)}, s32[4]{0:T(128)}, u32[]{:S(2)}) copy-start(s32[4]{0:T(128)} %lengths_ref.1) | copy-start | bytes 52
  2.1 21.7 %all-to-all-start = ((bf16[32,8,1024]{2,1,0:T(8,128)(2,1)}), bf16[32,8,1024]{2,1,0:T(8,128)(2,1)S(1)}, u32[]{:S(2)}, u32[]{:S(2)}) async-start(bf16[32,8,1024]{2,1,0:T(8,128)(2,1)} %bitcast.21), calls=%async_computation | async-start | bytes 1048576 | tf_op jit(solution)/shard_map/all_to_all | solution.py:382
  9.4 0.7 copy-start.8
  10.1 0.7 copy-start.14
  11.5 1.2 %copy-start.4 = (bf16[256,256]{1,0:T(8,128)(2,1)}, bf16[256,256]{1,0:T(8,128)(2,1)S(1)}, u32[]{:S(2)}) copy-start(bf16[256,256]{1,0:T(8,128)(2,1)S(1)} %get-tuple-element.30.unsort_ref) | copy-start | bytes 393220
  11.5 1.2 %copy-start.6 = (bf16[128,256]{1,0:T(8,128)(2,1)}, bf16[128,256]{1,0:T(8,128)(2,1)S(1)}, u32[]{:S(2)}) copy-start(bf16[128,256]{1,0:T(8,128)(2,1)S(1)} %get-tuple-element.27.back_ref) | copy-start | bytes 196612
  23.8 15.5 %collective-permute-start = (bf16[256,1024]{1,0:T(8,128)(2,1)}, bf16[256,1024]{1,0:T(8,128)(2,1)S(1)}, u32[]{:S(2)}, u32[]{:S(2)}) collective-permute-start(bf16[256,1024]{1,0:T(8,128)(2,1)} %pad_maximum_fusion), channel_id=1, source_target_pairs={{0,1},{1,0},{2,3},{3,2},{4,5},{5,4},{6,7},{7,6},{8,9},{9,8},{10,11... | collective-permute-start | bytes 1572872 | tf_op jit(solution)/shard_map/ppermute | solution.py:406
  26.3 0.9 copy-start.5
  27.2 29.8 %copy-start.2 = (bf16[1024,1024]{1,0:T(8,128)(2,1)S(1)}, bf16[1024,1024]{1,0:T(8,128)(2,1)}, u32[]{:S(2)}) copy-start(bf16[1024,1024]{1,0:T(8,128)(2,1)} %w_ref.3) | copy-start | bytes 6291460
  27.2 29.8 %copy-start.3 = (bf16[128,1024]{1,0:T(8,128)(2,1)S(1)}, bf16[128,1024]{1,0:T(8,128)(2,1)}, u32[]{:S(2)}) copy-start(bf16[128,1024]{1,0:T(8,128)(2,1)} %tokens_ref.1) | copy-start | bytes 786436
  27.2 29.8 %copy-start.9 = (f32[1024]{0:T(1024)S(1)}, f32[1024]{0:T(1024)}, u32[]{:S(2)}) copy-start(f32[1024]{0:T(1024)} %param.24) | copy-start | bytes 12292
  27.2 29.8 %copy-start.10 = (f32[1024]{0:T(1024)S(1)}, f32[1024]{0:T(1024)}, u32[]{:S(2)}) copy-start(f32[1024]{0:T(1024)} %param.25) | copy-start | bytes 12292
  39.3 17.7 %all-to-all-start.1 = ((bf16[32,8,1024]{2,1,0:T(8,128)(2,1)}), bf16[32,8,1024]{2,1,0:T(8,128)(2,1)S(1)}, u32[]{:S(2)}, u32[]{:S(2)}) async-start(bf16[32,8,1024]{2,1,0:T(8,128)(2,1)} %bitcast.7), calls=%async_computation.1 | async-start | bytes 1048576 | tf_op jit(solution)/shard_map/all_to_all | solution.py:450
  42.9 21.3 %collective-permute-start.4 = (bf16[256,1024]{1,0:T(8,128)(2,1)S(1)}, bf16[256,1024]{1,0:T(8,128)(2,1)}, u32[]{:S(2)}, u32[]{:S(2)}) collective-permute-start(bf16[256,1024]{1,0:T(8,128)(2,1)S(1)} %collective-permute-done.refs_0_), channel_id=1, source_target_pairs={{0,24},{4,28},{8,16},{12,20},{16,8},{20,12},{24,0},{28,4},{1,25},{... | collective-permute-start | bytes 1572872 | tf_op jit(solution)/shard_map/ppermute | solution.py:443
  45.4 28.9 %collective-permute-start.3 = (bf16[256,1024]{1,0:T(8,128)(2,1)S(1)}, bf16[256,1024]{1,0:T(8,128)(2,1)}, u32[]{:S(2)}, u32[]{:S(2)}) collective-permute-start(bf16[256,1024]{1,0:T(8,128)(2,1)S(1)} %collective-permute-done.refs_0_), channel_id=1, source_target_pairs={{0,16},{4,20},{8,24},{12,28},{16,0},{20,4},{24,8},{28,12},{1,17},{... | collective-permute-start | bytes 1572872 | tf_op jit(solution)/shard_map/ppermute | solution.py:443
  46.0 28.3 %collective-permute-start.2 = (bf16[256,1024]{1,0:T(8,128)(2,1)S(1)}, bf16[256,1024]{1,0:T(8,128)(2,1)}, u32[]{:S(2)}, u32[]{:S(2)}) collective-permute-start(bf16[256,1024]{1,0:T(8,128)(2,1)S(1)} %collective-permute-done.refs_0_), channel_id=1, source_target_pairs={{0,8},{4,12},{8,0},{12,4},{16,24},{20,28},{24,16},{28,20},{1,9},{5... | collective-permute-start | bytes 1572872 | tf_op jit(solution)/shard_map/ppermute | solution.py:443
  57.1 0.8 copy-start.7
  58.8 15.5 %collective-permute-start.5 = (bf16[64,1024]{1,0:T(8,128)(2,1)S(1)}, bf16[64,1024]{1,0:T(8,128)(2,1)S(1)}, u32[]{:S(2)}, u32[]{:S(2)}) collective-permute-start(bf16[64,1024]{1,0:T(8,128)(2,1)S(1)} %get-tuple-element.42), channel_id=1, source_target_pairs={{0,2},{2,0},{1,3},{3,1},{4,6},{6,4},{5,7},{7,5},{8,10},{10,8},{9,1... | collective-permute-start | bytes 393224 | tf_op jit(solution)/shard_map/ppermute | solution.py:500
  60.6 16.6 %collective-permute-start.1 = (bf16[256,1024]{1,0:T(8,128)(2,1)S(1)}, bf16[256,1024]{1,0:T(8,128)(2,1)S(1)}, u32[]{:S(2)}, u32[]{:S(2)}) collective-permute-start(bf16[256,1024]{1,0:T(8,128)(2,1)S(1)} %collective-permute-done.refs_0_), channel_id=1, source_target_pairs={{0,4},{4,0},{8,12},{12,8},{16,20},{20,16},{24,28},{28,24},{1,5},{5... | collective-permute-start | bytes 1572872 | tf_op jit(solution)/shard_map/ppermute | solution.py:443
  74.3 2.9 %collective-permute-start.6 = (bf16[256,1024]{1,0:T(8,128)(2,1)}, bf16[256,1024]{1,0:T(8,128)(2,1)S(1)}, u32[]{:S(2)}, u32[]{:S(2)}) collective-permute-start(bf16[256,1024]{1,0:T(8,128)(2,1)} %collective-permute-done.2.refs_2_), channel_id=1, source_target_pairs={{0,4},{4,0},{8,12},{12,8},{16,20},{20,16},{24,28},{28,24},{1,5},{5... | collective-permute-start | bytes 1572872 | tf_op jit(solution)/shard_map/ppermute | solution.py:443
  74.3 2.9 %collective-permute-start.7 = (bf16[256,1024]{1,0:T(8,128)(2,1)}, bf16[256,1024]{1,0:T(8,128)(2,1)S(1)}, u32[]{:S(2)}, u32[]{:S(2)}) collective-permute-start(bf16[256,1024]{1,0:T(8,128)(2,1)} %collective-permute-done.3.refs_4_), channel_id=1, source_target_pairs={{0,4},{4,0},{8,12},{12,8},{16,20},{20,16},{24,28},{28,24},{1,5},{5... | collective-permute-start | bytes 1572872 | tf_op jit(solution)/shard_map/ppermute | solution.py:443
  74.8 3.1 %collective-permute-start.8 = (bf16[256,1024]{1,0:T(8,128)(2,1)}, bf16[256,1024]{1,0:T(8,128)(2,1)S(1)}, u32[]{:S(2)}, u32[]{:S(2)}) collective-permute-start(bf16[256,1024]{1,0:T(8,128)(2,1)} %collective-permute-done.4.refs_6_), channel_id=1, source_target_pairs={{0,4},{4,0},{8,12},{12,8},{16,20},{20,16},{24,28},{28,24},{1,5},{5... | collective-permute-start | bytes 1572872 | tf_op jit(solution)/shard_map/ppermute | solution.py:443
  74.9 9.8 %collective-permute-start.10 = (bf16[64,1024]{1,0:T(8,128)(2,1)S(1)}, bf16[64,1024]{1,0:T(8,128)(2,1)S(1)}, u32[]{:S(2)}, u32[]{:S(2)}) collective-permute-start(bf16[64,1024]{1,0:T(8,128)(2,1)S(1)} %get-tuple-element.41), channel_id=1, source_target_pairs={{0,2},{2,0},{1,3},{3,1},{4,6},{6,4},{5,7},{7,5},{8,10},{10,8},{9,1... | collective-permute-start | bytes 393224 | tf_op jit(solution)/shard_map/ppermute | solution.py:500
  77.9 2.1 %copy-start = (bf16[1024,1024]{1,0:T(8,128)(2,1)S(1)}, bf16[1024,1024]{1,0:T(8,128)(2,1)}, u32[]{:S(2)}) copy-start(bf16[1024,1024]{1,0:T(8,128)(2,1)} %fc1_ref.5) | copy-start | bytes 6291460
  77.9 2.7 %copy-start.1 = (bf16[1024,1024]{1,0:T(8,128)(2,1)S(1)}, bf16[1024,1024]{1,0:T(8,128)(2,1)}, u32[]{:S(2)}) copy-start(bf16[1024,1024]{1,0:T(8,128)(2,1)} %fc2_ref.5) | copy-start | bytes 6291460
  82.2 12.9 %collective-permute-start.9 = (bf16[64,1024]{1,0:T(8,128)(2,1)S(1)}, bf16[64,1024]{1,0:T(8,128)(2,1)S(1)}, u32[]{:S(2)}, u32[]{:S(2)}) collective-permute-start(bf16[64,1024]{1,0:T(8,128)(2,1)S(1)} %ffn_whole.4), channel_id=1, source_target_pairs={{0,2},{2,0},{1,3},{3,1},{4,6},{6,4},{5,7},{7,5},{8,10},{10,8},{9,1... | collective-permute-start | bytes 393224 | tf_op jit(solution)/shard_map/ppermute | solution.py:500
  86.3 10.9 %copy-start.11 = (f32[1024]{0:T(1024)S(1)}, f32[1024]{0:T(1024)}, u32[]{:S(2)}) copy-start(f32[1024]{0:T(1024)} %param.26) | copy-start | bytes 12292
  86.3 10.9 %copy-start.12 = (f32[1024]{0:T(1024)S(1)}, f32[1024]{0:T(1024)}, u32[]{:S(2)}) copy-start(f32[1024]{0:T(1024)} %param.27) | copy-start | bytes 12292
  86.3 10.9 %collective-permute-start.11 = (bf16[64,1024]{1,0:T(8,128)(2,1)S(1)}, bf16[64,1024]{1,0:T(8,128)(2,1)S(1)}, u32[]{:S(2)}, u32[]{:S(2)}) collective-permute-start(bf16[64,1024]{1,0:T(8,128)(2,1)S(1)} %ffn_whole.5), channel_id=1, source_target_pairs={{0,2},{2,0},{1,3},{3,1},{4,6},{6,4},{5,7},{7,5},{8,10},{10,8},{9,1... | collective-permute-start | bytes 393224 | tf_op jit(solution)/shard_map/ppermute | solution.py:500

commit v5 on v4

--- a/solution.py
+++ b/solution.py
@@ -296,9 +296,8 @@
         copy.wait()
 
 
-def whole_kernel(x_ref, fc1_ref, fc2_ref, pair_fc1_ref, pair_fc2_ref, out_ref):
-    total = ffn_part(x_ref[...], fc1_ref[...], fc2_ref[...])
-    total += ffn_part(x_ref[...], pair_fc1_ref[...], pair_fc2_ref[...])
+def add_kernel(x_ref, base_ref, fc1_ref, fc2_ref, out_ref):
+    total = base_ref[...] + ffn_part(x_ref[...], fc1_ref[...], fc2_ref[...])
     out_ref[...] = total.astype(out_ref.dtype)
 
 
@@ -477,7 +476,7 @@
     def near_part(states):
         return pl.pallas_call(
             ffn_kernel,
-            out_shape=shape((tok_dev, width), jnp.float32),
+            out_shape=shape(states.shape, jnp.float32),
             in_specs=vmem(3),
             out_specs=vmem(1)[0],
             compiler_params=params(16 * 1024 * 1024),
@@ -500,14 +499,17 @@
         return lax.ppermute(states, "other", [(i, i ^ by) for i in range(others)])
 
     if by_permutes:
-        halves = 2
+        halves = 1
         half = tok_dev // halves
         visitors = [
             [shift(normed[i * half : (i + 1) * half], by) for i in range(halves)]
             for by in range(1, others)
         ]
-        shares, visitors[0][0] = lax.optimization_barrier((shares, visitors[0][0]))
+        own = near_part(normed)
+        shares, visitors, own = lax.optimization_barrier((shares, visitors, own))
         shares = [piece, mate] + [got for s in shares for got in (s, from_sharer(s, 1))]
+        bases = [[near_part(visitor) for visitor in some] for some in visitors]
+        shares, bases = lax.optimization_barrier((shares, bases))
         me_req = lax.axis_index("req").astype(jnp.int32).reshape(1)
         pair_weights = pl.pallas_call(
             assemble_kernel,
@@ -520,21 +522,22 @@
             name="assemble",
         )(me_req, *shares)
 
-        def whole(states, dtype):
+        def whole(states, base, dtype):
             return pl.pallas_call(
-                whole_kernel,
+                add_kernel,
                 out_shape=shape(states.shape, dtype),
-                in_specs=vmem(5),
+                in_specs=vmem(4),
                 out_specs=vmem(1)[0],
                 compiler_params=params(16 * 1024 * 1024),
                 cost_estimate=cost,
-                name="ffn_whole",
-            )(states, w_fc1, w_fc2, *pair_weights)
+                name="ffn_pair",
+            )(states, base, *pair_weights)
 
         parts = []
-        for by, pair_visitors in enumerate(visitors, 1):
-            parts += [shift(whole(visitor, jnp.bfloat16), by) for visitor in pair_visitors]
-        own = whole(normed, jnp.float32)
+        for by, (some, their) in enumerate(zip(visitors, bases), 1):
+            for visitor, base in zip(some, their):
+                parts.append(shift(whole(visitor, base, jnp.bfloat16), by))
+        own = whole(normed, own, jnp.float32)
     else:
         halves = 1
         pair = pair.reshape(sharers, -1, pair.shape[1])

time: 98.3 us -> 96.8 us (0.985)
  waiting for transfers between devices: 43.6 us -> 49.1 us
  starting transfers between devices: 25.3 us -> 20.8 us
  Pallas kernels: 23.1 us -> 21.9 us
    ppermute x4 -> x2, waiting for transfers between devices: 8.87 us -> 13.6 us  [shift(): return lax.ppermute(states, 'other', [(i, i ^ by) for i in range(others)])]
    ppermute x4 -> x2, starting transfers between devices: 7.29 us -> 3.41 us  [shift(): return lax.ppermute(states, 'other', [(i, i ^ by) for i in range(others)])]
    pallas_call x3 -> x4, Pallas kernels: 4.56 us -> 3.21 us  [the longest x2 1.62 us: near_part(): pl.pallas_call(ffn_kernel, out_shape=shape(states.shape, jnp.float32), in...]
    unnamed x30 -> x22, local copies, waits for them, and re-layouts: 3.92 us -> 3.2 us
  transfers between devices with their start and end apart: 14 -> 12, of which waited for: 7 -> 9; matrix products, arithmetic and copies ran while one was open for 2% -> 1% of each run, Pallas kernels for 20% -> 17%
where the time goes in v5:
time: 96.8 us; the launch traced here: 96.3 us
  waiting for transfers between devices  49.1 us (51%)
  Pallas kernels  21.9 us (23%)
  starting transfers between devices  20.8 us (21%)
  local copies, waits for them, and re-layouts  4.27 us (4%)
    ppermute x7, waiting for transfers between devices, from_sharer(): return lax.ppermute(piece, 'req', [(i, i ^ by) for i in range(sharers)])  13.6 us
    ppermute x2, waiting for transfers between devices, shift(): return lax.ppermute(states, 'other', [(i, i ^ by) for i in range(others)])  13.6 us
    pallas_call x1, Pallas kernels, per_device(): pl.pallas_call(attend_kernel, out_shape=shape((slots, width)), in_specs=s...  12.4 us
    all_to_all x1, waiting for transfers between devices, per_device(): lax.all_to_all(outgoing.reshape(devices, capacity, width), ALL, split_axi...  11.2 us
    all_to_all x1, waiting for transfers between devices, per_device(): lax.all_to_all(attended.reshape(devices, capacity, width), ALL, split_axi...  10.6 us
    all_to_all x1, starting transfers between devices, per_device(): lax.all_to_all(outgoing.reshape(devices, capacity, width), ALL, split_axi...  7.31 us
    ppermute x7, starting transfers between devices, from_sharer(): return lax.ppermute(piece, 'req', [(i, i ^ by) for i in range(sharers)])  4.57 us
    ppermute x2, starting transfers between devices, shift(): return lax.ppermute(states, 'other', [(i, i ^ by) for i in range(others)])  3.41 us
  transfers between devices with their start and end apart: 12, of which 9 were waited for; matrix products, arithmetic and copies ran while one was open for 1% of the time, Pallas kernels for 17%

profile of v5, /device:TPU:0, one launch (start us, length us, event | category | flops | bytes accessed | tf_op | source)
XLA Modules:
  0.0 96.3 jit_solution(16668554815466159021)
XLA Ops:
  0.0 2.1 %dispatch.1 = bf16[256,1024]{1,0:T(8,128)(2,1)} custom-call(s32[1]{0:T(128)} %bitcast.2.me_ref, s32[32,128]{1,0:T(8,128)} %bitcast.14, bf16[128,1024]{1,0:T(8,128)(2,1)} %tokens_ref.1), custom_call_target="tpu_custom_call" | custom-call | tf_op jit(solution)/shard_map/dispatch/pallas_call | solution.py:368
  2.1 7.3 %all-to-all-start = ((bf16[32,8,1024]{2,1,0:T(8,128)(2,1)}), bf16[32,8,1024]{2,1,0:T(8,128)(2,1)S(1)}, u32[]{:S(2)}, u32[]{:S(2)}) async-start(bf16[32,8,1024]{2,1,0:T(8,128)(2,1)} %bitcast.21), calls=%async_computation | async-start | bytes 1048576 | tf_op jit(solution)/shard_map/all_to_all | solution.py:381
  9.4 0.7 copy-done.4
  10.1 0.7 copy-done.10
  10.9 0.6 table.1
  11.5 1.1 %constant_dynamic-slice_fusion = (bf16[128,1024]{1,0:T(8,128)(2,1)S(1)}, bf16[128,1024]{1,0:T(8,128)(2,1)S(1)}) fusion(bf16[1024,1024]{1,0:T(8,128)(2,1)} %fc2_ref.3, s32[]{:T(128)S(6)} %select_n.4, bf16[1024,1024]{1,0:T(8,128)(2,1)} %fc1_ref.3), kind=kLoop, calls=%fused_computation.1 | loop fusion | bytes 1048580 | tf_op jit(solution)/shard_map/dynamic_slice | solution.py:316
  12.6 11.2 %all-to-all-done = bf16[32,8,1024]{2,1,0:T(8,128)(2,1)S(1)} async-done(((bf16[32,8,1024]{2,1,0:T(8,128)(2,1)}), bf16[32,8,1024]{2,1,0:T(8,128)(2,1)S(1)}, u32[]{:S(2)}, u32[]{:S(2)}) %all-to-all-start) | async-done | bytes 524320 | tf_op jit(solution)/shard_map/all_to_all | solution.py:381
  23.8 2.5 %collective-permute-start = (bf16[256,1024]{1,0:T(8,128)(2,1)S(1)}, bf16[256,1024]{1,0:T(8,128)(2,1)S(1)}, u32[]{:S(2)}, u32[]{:S(2)}) collective-permute-start(bf16[256,1024]{1,0:T(8,128)(2,1)S(1)} %pad_maximum_fusion), channel_id=1, source_target_pairs={{0,1},{1,0},{2,3},{3,2},{4,5},{5,4},{6,7},{7,6},{8,9},{9,8},{10,11... | collective-permute-start | bytes 1572872 | tf_op jit(solution)/shard_map/ppermute | solution.py:405
  26.3 12.4 %attend.1 = bf16[256,1024]{1,0:T(8,128)(2,1)} custom-call(s32[8,128]{1,0:T(8,128)S(1)} %get-tuple-element.38.starts_ref, s32[4]{0:T(128)S(1)} %copy-done.9, bf16[256,256]{1,0:T(8,128)(2,1)S(1)} %get-tuple-element.39.sort_ref, bf16[256,256]{1,0:T(8,128)(2,1)S(1)} %get-tuple-element.40.unsort_ref, bf16[256,1024]{1,0:T(8,128)(2,1)S(1)} %bitcast.13, ...), custom_call_target="tpu_custom_call" | custom-call | flops 4294967296 | bytes 20000000 | tf_op jit(solution)/shard_map/attend/pallas_call | solution.py:406
  38.8 2.9 %all-to-all-start.1 = ((bf16[32,8,1024]{2,1,0:T(8,128)(2,1)}), bf16[32,8,1024]{2,1,0:T(8,128)(2,1)S(1)}, u32[]{:S(2)}, u32[]{:S(2)}) async-start(bf16[32,8,1024]{2,1,0:T(8,128)(2,1)} %bitcast.7), calls=%async_computation.1 | async-start | bytes 1048576 | tf_op jit(solution)/shard_map/all_to_all | solution.py:449
  41.7 2.5 %collective-permute-start.3 = (bf16[256,1024]{1,0:T(8,128)(2,1)S(1)}, bf16[256,1024]{1,0:T(8,128)(2,1)}, u32[]{:S(2)}, u32[]{:S(2)}) collective-permute-start(bf16[256,1024]{1,0:T(8,128)(2,1)S(1)} %collective-permute-done.refs_0_), channel_id=1, source_target_pairs={{0,24},{4,28},{8,16},{12,20},{16,8},{20,12},{24,0},{28,4},{1,25},{... | collective-permute-start | bytes 1572872 | tf_op jit(solution)/shard_map/ppermute | solution.py:442
  44.2 0.5 collective-permute-start.2
  44.7 0.6 collective-permute-start.1
  45.3 10.6 %all-to-all-done.1 = bf16[32,8,1024]{2,1,0:T(8,128)(2,1)S(1)} async-done(((bf16[32,8,1024]{2,1,0:T(8,128)(2,1)}), bf16[32,8,1024]{2,1,0:T(8,128)(2,1)S(1)}, u32[]{:S(2)}, u32[]{:S(2)}) %all-to-all-start.1) | async-done | bytes 524320 | tf_op jit(solution)/shard_map/all_to_all | solution.py:449
  55.9 1.7 %copy-done.2 = bf16[1024,1024]{1,0:T(8,128)(2,1)S(1)} copy-done((bf16[1024,1024]{1,0:T(8,128)(2,1)S(1)}, bf16[1024,1024]{1,0:T(8,128)(2,1)}, u32[]{:S(2)}) %copy-start.2) | copy-done | bytes 2097176
  57.7 0.8 out_norm.1.x_ref.normed_ref
  58.5 1.9 %collective-permute-start.4 = (bf16[128,1024]{1,0:T(8,128)(2,1)S(1)}, bf16[128,1024]{1,0:T(8,128)(2,1)S(1)}, u32[]{:S(2)}, u32[]{:S(2)}) collective-permute-start(bf16[128,1024]{1,0:T(8,128)(2,1)S(1)} %out_norm.1.x_ref.normed_ref), channel_id=1, source_target_pairs={{0,2},{2,0},{1,3},{3,1},{4,6},{6,4},{5,7},{7,5},{8,10},{10,8},{9,1... | collective-permute-start | bytes 786440 | tf_op jit(solution)/shard_map/ppermute | solution.py:499
  60.8 0.8 ffn_near.2.base_ref
  61.6 1.4 %collective-permute-done.3.refs_6_ = bf16[256,1024]{1,0:T(8,128)(2,1)} collective-permute-done((bf16[256,1024]{1,0:T(8,128)(2,1)S(1)}, bf16[256,1024]{1,0:T(8,128)(2,1)}, u32[]{:S(2)}, u32[]{:S(2)}) %collective-permute-start.3) | collective-permute-done | bytes 524320 | tf_op jit(solution)/shard_map/ppermute | solution.py:442
  63.0 10.1 %collective-permute-done.2.refs_4_ = bf16[256,1024]{1,0:T(8,128)(2,1)} collective-permute-done((bf16[256,1024]{1,0:T(8,128)(2,1)S(1)}, bf16[256,1024]{1,0:T(8,128)(2,1)}, u32[]{:S(2)}, u32[]{:S(2)}) %collective-permute-start.2) | collective-permute-done | bytes 524320 | tf_op jit(solution)/shard_map/ppermute | solution.py:442
  73.0 1.0 %collective-permute-done.4.x_ref = bf16[128,1024]{1,0:T(8,128)(2,1)S(1)} collective-permute-done((bf16[128,1024]{1,0:T(8,128)(2,1)S(1)}, bf16[128,1024]{1,0:T(8,128)(2,1)S(1)}, u32[]{:S(2)}, u32[]{:S(2)}) %collective-permute-start.4) | collective-permute-done | bytes 262176 | tf_op jit(solution)/shard_map/ppermute | solution.py:499
  74.2 0.4 collective-permute-start.7
  74.7 0.8 ffn_near.3.base_ref
  75.5 0.7 collective-permute-done.6.refs_3_
  76.2 0.7 collective-permute-done.7.refs_5_
  76.9 0.7 collective-permute-done.8.refs_7_
  77.7 1.8 %assemble.1 = (bf16[1024,1024]{1,0:T(8,128)(2,1)S(1)}, bf16[1024,1024]{1,0:T(8,128)(2,1)S(1)}) custom-call(s32[1]{0:T(128)} %bitcast.11.me_ref, bf16[256,1024]{1,0:T(8,128)(2,1)S(1)} %collective-permute-done.refs_0_, bf16[256,1024]{1,0:T(8,128)(2,1)S(1)} %collective-permute-done.5.refs_1_, bf16[256,1024]{1,0:T(8,128)(2,1)} %collective-permute-done.1.refs_2_, ...), custom_call_target="tpu_custom_call" | custom-call | flops 536870912 | bytes 4194304 | tf_op jit(solution)/shard_map/assemble/pallas_call | solution.py:514
  79.5 0.8 ffn_pair.3
  80.4 1.5 %collective-permute-start.9 = (bf16[128,1024]{1,0:T(8,128)(2,1)S(1)}, bf16[128,1024]{1,0:T(8,128)(2,1)S(1)}, u32[]{:S(2)}, u32[]{:S(2)}) collective-permute-start(bf16[128,1024]{1,0:T(8,128)(2,1)S(1)} %ffn_pair.3), channel_id=1, source_target_pairs={{0,2},{2,0},{1,3},{3,1},{4,6},{6,4},{5,7},{7,5},{8,10},{10,8},{9,1... | collective-permute-start | bytes 786440 | tf_op jit(solution)/shard_map/ppermute | solution.py:499
  81.9 0.8 ffn_pair.2.own_ref
  82.7 12.6 %collective-permute-done.9.refs_0_ = bf16[128,1024]{1,0:T(8,128)(2,1)S(1)} collective-permute-done((bf16[128,1024]{1,0:T(8,128)(2,1)S(1)}, bf16[128,1024]{1,0:T(8,128)(2,1)S(1)}, u32[]{:S(2)}, u32[]{:S(2)}) %collective-permute-start.9) | collective-permute-done | bytes 262176 | tf_op jit(solution)/shard_map/ppermute | solution.py:499
  95.3 1.0 %final_norm.1 = bf16[128,1024]{1,0:T(8,128)(2,1)} custom-call(f32[1,1024]{1,0:T(1,128)S(1)} %bitcast.18, f32[1,1024]{1,0:T(1,128)S(1)} %bitcast.19, bf16[128,1024]{1,0:T(8,128)(2,1)S(1)} %out_norm.1.x_ref.normed_ref, f32[128,1024]{1,0:T(8,128)S(1)} %ffn_pair.2.own_ref, bf16[128,1024]{1,0:T(8,128)(2,1)S(1)} %collective-permute-done.9.refs_0_), custom_call_target="tpu_custom_call" | custom-call | tf_op jit(solution)/shard_map/final_norm/pallas_call | solution.py:554
  (26 shorter events, 0.7 us)
Async XLA Ops:
  0.0 26.3 %copy-start.9 = (s32[4]{0:T(128)S(1)}, s32[4]{0:T(128)}, u32[]{:S(2)}) copy-start(s32[4]{0:T(128)} %lengths_ref.1) | copy-start | bytes 52
  2.1 21.7 %all-to-all-start = ((bf16[32,8,1024]{2,1,0:T(8,128)(2,1)}), bf16[32,8,1024]{2,1,0:T(8,128)(2,1)S(1)}, u32[]{:S(2)}, u32[]{:S(2)}) async-start(bf16[32,8,1024]{2,1,0:T(8,128)(2,1)} %bitcast.21), calls=%async_computation | async-start | bytes 1048576 | tf_op jit(solution)/shard_map/all_to_all | solution.py:381
  9.4 0.7 copy-start.4
  10.1 0.7 copy-start.10
  23.8 15.0 %collective-permute-start = (bf16[256,1024]{1,0:T(8,128)(2,1)S(1)}, bf16[256,1024]{1,0:T(8,128)(2,1)S(1)}, u32[]{:S(2)}, u32[]{:S(2)}) collective-permute-start(bf16[256,1024]{1,0:T(8,128)(2,1)S(1)} %pad_maximum_fusion), channel_id=1, source_target_pairs={{0,1},{1,0},{2,3},{3,2},{4,5},{5,4},{6,7},{7,6},{8,9},{9,8},{10,11... | collective-permute-start | bytes 1572872 | tf_op jit(solution)/shard_map/ppermute | solution.py:405
  26.3 29.6 %copy-start.3 = (bf16[128,1024]{1,0:T(8,128)(2,1)S(1)}, bf16[128,1024]{1,0:T(8,128)(2,1)}, u32[]{:S(2)}) copy-start(bf16[128,1024]{1,0:T(8,128)(2,1)} %tokens_ref.1) | copy-start | bytes 786436
  26.3 29.6 %copy-start.5 = (f32[1024]{0:T(1024)S(1)}, f32[1024]{0:T(1024)}, u32[]{:S(2)}) copy-start(f32[1024]{0:T(1024)} %param.24) | copy-start | bytes 12292
  26.3 29.6 %copy-start.6 = (f32[1024]{0:T(1024)S(1)}, f32[1024]{0:T(1024)}, u32[]{:S(2)}) copy-start(f32[1024]{0:T(1024)} %param.25) | copy-start | bytes 12292
  38.8 22.0 %copy-start = (bf16[1024,1024]{1,0:T(8,128)(2,1)S(1)}, bf16[1024,1024]{1,0:T(8,128)(2,1)}, u32[]{:S(2)}) copy-start(bf16[1024,1024]{1,0:T(8,128)(2,1)} %fc1_ref.3) | copy-start | bytes 6291460
  38.8 17.1 %all-to-all-start.1 = ((bf16[32,8,1024]{2,1,0:T(8,128)(2,1)}), bf16[32,8,1024]{2,1,0:T(8,128)(2,1)S(1)}, u32[]{:S(2)}, u32[]{:S(2)}) async-start(bf16[32,8,1024]{2,1,0:T(8,128)(2,1)} %bitcast.7), calls=%async_computation.1 | async-start | bytes 1048576 | tf_op jit(solution)/shard_map/all_to_all | solution.py:449
  41.7 21.3 %collective-permute-start.3 = (bf16[256,1024]{1,0:T(8,128)(2,1)S(1)}, bf16[256,1024]{1,0:T(8,128)(2,1)}, u32[]{:S(2)}, u32[]{:S(2)}) collective-permute-start(bf16[256,1024]{1,0:T(8,128)(2,1)S(1)} %collective-permute-done.refs_0_), channel_id=1, source_target_pairs={{0,24},{4,28},{8,16},{12,20},{16,8},{20,12},{24,0},{28,4},{1,25},{... | collective-permute-start | bytes 1572872 | tf_op jit(solution)/shard_map/ppermute | solution.py:442
  44.2 28.9 %collective-permute-start.2 = (bf16[256,1024]{1,0:T(8,128)(2,1)S(1)}, bf16[256,1024]{1,0:T(8,128)(2,1)}, u32[]{:S(2)}, u32[]{:S(2)}) collective-permute-start(bf16[256,1024]{1,0:T(8,128)(2,1)S(1)} %collective-permute-done.refs_0_), channel_id=1, source_target_pairs={{0,16},{4,20},{8,24},{12,28},{16,0},{20,4},{24,8},{28,12},{1,17},{... | collective-permute-start | bytes 1572872 | tf_op jit(solution)/shard_map/ppermute | solution.py:442
  44.7 28.3 %collective-permute-start.1 = (bf16[256,1024]{1,0:T(8,128)(2,1)S(1)}, bf16[256,1024]{1,0:T(8,128)(2,1)}, u32[]{:S(2)}, u32[]{:S(2)}) collective-permute-start(bf16[256,1024]{1,0:T(8,128)(2,1)S(1)} %collective-permute-done.refs_0_), channel_id=1, source_target_pairs={{0,8},{4,12},{8,0},{12,4},{16,24},{20,28},{24,16},{28,20},{1,9},{5... | collective-permute-start | bytes 1572872 | tf_op jit(solution)/shard_map/ppermute | solution.py:442
  55.9 4.8 %copy-start.1 = (bf16[1024,1024]{1,0:T(8,128)(2,1)S(1)}, bf16[1024,1024]{1,0:T(8,128)(2,1)}, u32[]{:S(2)}) copy-start(bf16[1024,1024]{1,0:T(8,128)(2,1)} %fc2_ref.3) | copy-start | bytes 6291460
  55.9 1.7 %copy-start.2 = (bf16[1024,1024]{1,0:T(8,128)(2,1)S(1)}, bf16[1024,1024]{1,0:T(8,128)(2,1)}, u32[]{:S(2)}) copy-start(bf16[1024,1024]{1,0:T(8,128)(2,1)} %w_ref.3) | copy-start | bytes 6291460
  58.5 15.6 %collective-permute-start.4 = (bf16[128,1024]{1,0:T(8,128)(2,1)S(1)}, bf16[128,1024]{1,0:T(8,128)(2,1)S(1)}, u32[]{:S(2)}, u32[]{:S(2)}) collective-permute-start(bf16[128,1024]{1,0:T(8,128)(2,1)S(1)} %out_norm.1.x_ref.normed_ref), channel_id=1, source_target_pairs={{0,2},{2,0},{1,3},{3,1},{4,6},{6,4},{5,7},{7,5},{8,10},{10,8},{9,1... | collective-permute-start | bytes 786440 | tf_op jit(solution)/shard_map/ppermute | solution.py:499
  60.4 15.2 %collective-permute-start.5 = (bf16[256,1024]{1,0:T(8,128)(2,1)S(1)}, bf16[256,1024]{1,0:T(8,128)(2,1)S(1)}, u32[]{:S(2)}, u32[]{:S(2)}) collective-permute-start(bf16[256,1024]{1,0:T(8,128)(2,1)S(1)} %collective-permute-done.refs_0_), channel_id=1, source_target_pairs={{0,4},{4,0},{8,12},{12,8},{16,20},{20,16},{24,28},{28,24},{1,5},{5... | collective-permute-start | bytes 1572872 | tf_op jit(solution)/shard_map/ppermute | solution.py:442
  74.1 2.1 %collective-permute-start.6 = (bf16[256,1024]{1,0:T(8,128)(2,1)}, bf16[256,1024]{1,0:T(8,128)(2,1)S(1)}, u32[]{:S(2)}, u32[]{:S(2)}) collective-permute-start(bf16[256,1024]{1,0:T(8,128)(2,1)} %collective-permute-done.1.refs_2_), channel_id=1, source_target_pairs={{0,4},{4,0},{8,12},{12,8},{16,20},{20,16},{24,28},{28,24},{1,5},{5... | collective-permute-start | bytes 1572872 | tf_op jit(solution)/shard_map/ppermute | solution.py:442
  74.2 2.8 %collective-permute-start.7 = (bf16[256,1024]{1,0:T(8,128)(2,1)}, bf16[256,1024]{1,0:T(8,128)(2,1)S(1)}, u32[]{:S(2)}, u32[]{:S(2)}) collective-permute-start(bf16[256,1024]{1,0:T(8,128)(2,1)} %collective-permute-done.2.refs_4_), channel_id=1, source_target_pairs={{0,4},{4,0},{8,12},{12,8},{16,20},{20,16},{24,28},{28,24},{1,5},{5... | collective-permute-start | bytes 1572872 | tf_op jit(solution)/shard_map/ppermute | solution.py:442
  74.6 3.1 %collective-permute-start.8 = (bf16[256,1024]{1,0:T(8,128)(2,1)}, bf16[256,1024]{1,0:T(8,128)(2,1)S(1)}, u32[]{:S(2)}, u32[]{:S(2)}) collective-permute-start(bf16[256,1024]{1,0:T(8,128)(2,1)} %collective-permute-done.3.refs_6_), channel_id=1, source_target_pairs={{0,4},{4,0},{8,12},{12,8},{16,20},{20,16},{24,28},{28,24},{1,5},{5... | collective-permute-start | bytes 1572872 | tf_op jit(solution)/shard_map/ppermute | solution.py:442
  80.3 15.0 %copy-start.7 = (f32[1024]{0:T(1024)S(1)}, f32[1024]{0:T(1024)}, u32[]{:S(2)}) copy-start(f32[1024]{0:T(1024)} %param.26) | copy-start | bytes 12292
  80.3 15.0 %copy-start.8 = (f32[1024]{0:T(1024)S(1)}, f32[1024]{0:T(1024)}, u32[]{:S(2)}) copy-start(f32[1024]{0:T(1024)} %param.27) | copy-start | bytes 12292
  80.4 14.9 %collective-permute-start.9 = (bf16[128,1024]{1,0:T(8,128)(2,1)S(1)}, bf16[128,1024]{1,0:T(8,128)(2,1)S(1)}, u32[]{:S(2)}, u32[]{:S(2)}) collective-permute-start(bf16[128,1024]{1,0:T(8,128)(2,1)S(1)} %ffn_pair.3), channel_id=1, source_target_pairs={{0,2},{2,0},{1,3},{3,1},{4,6},{6,4},{5,7},{7,5},{8,10},{10,8},{9,1... | collective-permute-start | bytes 786440 | tf_op jit(solution)/shard_map/ppermute | solution.py:499
